TPU v7x, 32 devices: a whole 2x2x4 slice. The times are simulated.
32 devices in a mesh: grp: 2 (over y), ctx: 4 (over z), head: 4 (over x, core).
Axes of the slice: x: 2, y: 2, z: 4, core: 2. Of those that a mesh axis runs over, the one named last changes fastest.
Arguments:
- behavior_embed: bfloat16 [4, 2048, 256], P('grp', 'ctx'), parts along dimension 0, may hold values from -6 to 6
- behavior_mask: int32 [4, 2048], P('grp', 'ctx'), parts along dimension 0, may hold values 0 or 1
- history_len: int32 [4], P('grp'), parts along dimension 0, may hold values from 256 to 2048, as said below
- log_decay: float32 [8, 4, 2048], P('head', 'grp', 'ctx'), parts along dimension 1, may hold values from -2 to 0
- candidate_embed: bfloat16 [4, 512, 256], P('grp', 'ctx'), parts along dimension 0, may hold values from -6 to 6
- input_weight: bfloat16 [256, 1024], replicated, may hold values from -0.375 to 0.375
- input_gain: float32 [1024], replicated, may hold values from 0.5 to 1.5
- proj_weight: bfloat16 [4, 1024, 1024], P(None, None, 'head'), may hold values from -0.1875 to 0.1875
- output_gain: float32 [1024], P('head'), may hold values from 0.5 to 1.5
- ranker_first: bfloat16 [1024, 1024], P('head'), may hold values from -0.1875 to 0.1875
- ranker_second: bfloat16 [1024], replicated, may hold values from -0.1875 to 0.1875
Outputs:
- history_out: bfloat16 [4, 2048, 1024], P('grp', 'ctx', 'head'), parts along dimension 0
- scores: float32 [4, 512], P('grp', ('ctx', 'head')), parts along dimension 0
There are 2 independent parts, one for each index of `grp`. A program takes and returns all parts, laid end to end along the dimension named above; an argument that names none is the same for every part. Nothing has to cross between parts.
Inputs may be any that keep to these rules, and one draw needn't show every extreme that they name: Histories are padded at the start: the last history_len[u] positions hold user u's behaviors; at least one user's history fills all 2048 positions.
All inputs are finite; a program needn't handle non-finite values. No bound on the sum of `behavior_mask` on one device may be relied on, other than what follows from the above.
Results may differ from a plain program's by a relative error of at most 0.0098.
Values may be sent and summed in bfloat16 or wider, within the bound.
A program may use at most 64 MiB of HBM per device.

v0:
```python
import jax
import jax.numpy as jnp
from jax import lax
from jax.sharding import PartitionSpec as P

DH = 128


epsilon = 1e-05
highest = lax.Precision.HIGHEST


def rms_norm(values, gain_row):
    mean_square = jnp.mean(values * values, axis=-1, keepdims=True)
    return values * lax.rsqrt(mean_square + epsilon) * gain_row


def local(
    behavior_embed,
    behavior_mask,
    history_len,
    log_decay,
    candidate_embed,
    input_weight,
    input_gain,
    proj_weight,
    output_gain,
    ranker_first,
    ranker_second,
):
    user_count, span_len = behavior_mask.shape
    cand_len = candidate_embed.shape[1]
    embed_width = behavior_embed.shape[2]
    head_cols = proj_weight.shape[2]
    heads_here = head_cols // DH
    ctx_count = lax.axis_size("ctx")
    ctx_index = lax.axis_index("ctx")
    head_count = lax.axis_size("head")
    head_index = lax.axis_index("head")
    seq_total = span_len * ctx_count
    position_indices = ctx_index * span_len + jnp.arange(span_len, dtype=jnp.int32)
    valid_mask = (
        (position_indices[None, :] >= seq_total - history_len[:, None]) & (behavior_mask == 1)
    ).astype(jnp.float32)
    behavior_rows = behavior_embed.reshape(user_count * span_len, embed_width)
    candidate_rows = jnp.transpose(candidate_embed, (1, 0, 2)).reshape(
        cand_len * user_count, embed_width
    )
    behavior_raw = lax.optimization_barrier(
        jnp.dot(behavior_rows, input_weight, preferred_element_type=jnp.float32).astype(
            jnp.bfloat16
        )
    )
    candidate_raw = lax.optimization_barrier(
        jnp.dot(candidate_rows, input_weight, preferred_element_type=jnp.float32).astype(
            jnp.bfloat16
        )
    )
    behavior_norm = rms_norm(behavior_raw.astype(jnp.float32), input_gain).astype(jnp.bfloat16)
    candidate_norm = rms_norm(candidate_raw.astype(jnp.float32), input_gain).astype(jnp.bfloat16)
    projected = jnp.einsum(
        "rd,pdc->prc", behavior_norm, proj_weight, preferred_element_type=jnp.float32
    )
    head_shape = (user_count, span_len, heads_here, DH)
    query_rows = projected[0].astype(jnp.bfloat16).reshape(head_shape)
    key_rows = (projected[1] * DH ** (-0.5)).astype(jnp.bfloat16).reshape(head_shape)
    value_rows = projected[2].astype(jnp.bfloat16).reshape(head_shape)
    gate_rows = projected[3].astype(jnp.bfloat16).reshape(head_shape)
    cumulative = jnp.cumsum(log_decay, axis=-1)
    span_total = cumulative[..., -1]
    row_ids = jnp.arange(span_len)
    causal = row_ids[:, None] >= row_ids[None, :]
    log_gap = cumulative[..., :, None] - cumulative[..., None, :]
    decay_matrix = (
        jnp.where(causal, jnp.exp(jnp.where(causal, log_gap, 0.0)), 0.0)
        * valid_mask[None, :, None, :]
    )
    scores_local = jnp.einsum(
        "uihd,ujhd->huij", query_rows, key_rows, preferred_element_type=jnp.float32
    )
    value_wide = value_rows.astype(jnp.float32)
    within = jnp.einsum(
        "huij,ujhd->uihd", scores_local * decay_matrix, value_wide, precision=highest
    )
    key_weight = jnp.exp(span_total[..., None] - cumulative) * valid_mask[None]
    local_state = jnp.einsum(
        "ujhd,ujhe->hude",
        key_rows.astype(jnp.float32) * jnp.transpose(key_weight, (1, 2, 0))[..., None],
        value_wide,
        precision=highest,
    )
    log_rows = lax.all_gather(span_total[None], "ctx", axis=0, tiled=True)
    through = jnp.cumsum(log_rows, axis=0)
    device_ids = jnp.arange(ctx_count)
    before_self = jnp.sum(jnp.where(device_ids[:, None, None] < ctx_index, log_rows, 0.0), axis=0)
    all_logs = jnp.sum(log_rows, axis=0)
    shard_piece = lax.all_gather(local_state[None], "ctx", axis=0, tiled=True)
    piece_len = shard_piece.shape[0]
    owners = jnp.arange(piece_len)
    weight_in = jnp.where(
        owners[:, None, None] < ctx_index,
        jnp.exp(jnp.minimum(before_self[None] - through, 0.0)),
        0.0,
    )
    weight_end = jnp.exp(jnp.minimum(all_logs[None] - through, 0.0))
    state_in = jnp.einsum("phu,phude->hude", weight_in, shard_piece, precision=highest)
    final_full = jnp.einsum("phu,phude->hude", weight_end, shard_piece, precision=highest)
    final_state = final_full.astype(jnp.bfloat16)
    carried = (
        jnp.einsum("uihd,hude->uihe", query_rows.astype(jnp.float32), state_in, precision=highest)
        * jnp.exp(jnp.transpose(cumulative, (1, 2, 0)))[..., None]
    )
    readout = within + carried
    gain_heads = output_gain.reshape(heads_here, DH)
    history_out = (
        (rms_norm(readout, gain_heads) * jax.nn.silu(gate_rows.astype(jnp.float32)))
        .reshape(user_count, span_len, head_cols)
        .astype(jnp.bfloat16)
    )
    candidate_query = (
        jnp.dot(candidate_norm, proj_weight[0], preferred_element_type=jnp.float32)
        .astype(jnp.bfloat16)
        .reshape(cand_len, user_count, heads_here, DH)
    )
    candidate_read = jnp.einsum(
        "cuhd,hude->cuhe", candidate_query, final_state, preferred_element_type=jnp.float32
    )
    own_cols = lax.dynamic_slice_in_dim(candidate_norm, head_index * head_cols, head_cols, 1)
    candidate_feat = (
        rms_norm(candidate_read, gain_heads).reshape(cand_len * user_count, head_cols)
        + own_cols.astype(jnp.float32)
    ).astype(jnp.bfloat16)
    share_rows = cand_len * user_count // head_count
    summed = lax.psum(
        jnp.dot(candidate_feat, ranker_first, preferred_element_type=jnp.float32), "head"
    )
    hidden = lax.dynamic_slice_in_dim(summed, head_index * share_rows, share_rows, 0)
    scores = jnp.dot(jax.nn.silu(hidden), ranker_second.astype(jnp.float32), precision=highest)
    scores = scores.reshape(cand_len // head_count, user_count).T
    return (history_out, scores)


def solution(mesh):
    in_specs = (
        P("grp", "ctx", None),
        P("grp", "ctx"),
        P("grp"),
        P("head", "grp", "ctx"),
        P("grp", "ctx", None),
        P(),
        P(),
        P(None, None, "head"),
        P("head"),
        P("head", None),
        P(),
    )
    out_specs = (P("grp", "ctx", "head"), P("grp", ("ctx", "head")))
    return jax.shard_map(local, mesh=mesh, in_specs=in_specs, out_specs=out_specs, check_vma=False)
```

profile of v0, /device:TPU:0, one launch (start us, length us, event | category | flops | bytes accessed | tf_op | source)
XLA Modules:
  0.0 99.0 jit_solution(13549878280901394313)
XLA Ops:
  7.2 0.0 copy-start
  7.2 0.0 copy-start.12
  7.2 0.0 copy-start.8
  7.2 0.0 all-gather.4.cloned.1.call-start
  7.3 1.0 copy-done
  8.2 1.8 %convolution_convert_fusion = bf16[1024,1024]{1,0:T(8,128)(2,1)S(1)} fusion(bf16[1024,256]{1,0:T(8,128)(2,1)S(1)} %bitcast.59, bf16[256,1024]{1,0:T(8,128)(2,1)} %param.16), kind=kOutput, calls=%fused_computation.22 | convolution fusion | flops 537919488 | bytes 3145728 | tf_op jit(solution)/shard_map/dot_general | solution.py:50
  10.0 0.5 fusion.1
  10.5 2.4 %fusion.69 = (bf16[4,1024,256]{2,1,0:T(8,128)(2,1)S(1)}, f32[4,1024,256]{2,1,0:T(8,128)S(1)}) fusion(bf16[4,1024,256]{2,1,0:T(8,128)(2,1)S(1)} %copy-done.12, bf16[1024,1024]{1,0:T(8,128)(2,1)S(1)} %convolution_convert_fusion, f32[1024]{0:T(1024)S(1)} %copy-done.8, f32[1024]{0:T(1024)S(1)} %add_rsqrt_fusion.1), kind=kOutput, calls=%fused_computation.100 | convolution fusion | flops 2152726528 | bytes 10493952 | tf_op jit(solution)/shard_map/rd,pdc->prc/dot_general | solution.py:61
  12.9 0.0 copy-start.13
  12.9 0.0 copy-start.7
  12.9 0.0 copy-start.10
  12.9 0.9 fusion.68
  13.9 0.1 fusion.33
  14.0 0.1 convert_element_type.77
  14.2 1.2 %reduce-window.6 = f32[2,2,4,128]{3,2,1,0:T(4,128)S(1)} reduce-window(f32[2,2,4,128]{3,2,1,0:T(4,128)S(1)} %reshape.123, f32[]{:T(128)} %constant.15.clone.1), window={size=1x1x1x128 pad=0_0x0_0x0_0x127_0}, to_apply=%region_1.0 | reduce-window | flops 260096 | bytes 16388 | tf_op jit(solution)/shard_map/reduce-window
  15.4 0.2 slice_reduce_fusion
  15.6 0.3 reduce-window.9
  15.9 0.1 broadcast_add_fusion
  16.0 0.1 convert_element_type.74
  16.1 0.0 copy-start.11
  16.2 0.0 copy-start.3
  16.2 0.4 copy.51
  16.6 0.1 slice.40
  16.7 0.1 copy.82
  16.8 0.1 and_convert_fusion
  16.8 0.1 multiply_bitcast_fusion
  16.9 1.4 %fusion.34 = f32[2,2,128,128]{3,2,1,0:T(8,128)} fusion(bf16[2,512,2,128]{1,3,0,2:T(8,128)(2,1)S(1)} %copy.51, bf16[2,512,2,128]{3,2,1,0:T(2,128)(2,1)S(1)} %convert_element_type.74, f32[2,512,2]{1,0,2:T(2,128)S(1)} %multiply_bitcast_fusion), kind=kOutput, calls=%fused_computation.47 | convolution fusion | flops 403177472 | bytes 1318912 | tf_op jit(solution)/shard_map/ujhd,ujhe->hude/dot_general | solution.py:86
  18.4 0.0 all-gather.4.cloned.1.call-update
  18.4 0.0 all-reduce.2.cloned.1.call-start
  18.5 12.8 %all-gather = f32[8,2,1]{1,2,0:T(1,128)S(1)} all-gather(f32[2,2,1]{1,2,0:T(1,128)S(1)} %copy.82), channel_id=2, replica_groups=mesh['grp'=2,'ctx'=4,'head'=4] {'ctx'}, dimensions={0}, use_global_device_ids=true | all-gather | bytes 80 | tf_op jit(solution)/shard_map/all_gather | solution.py:92
  31.3 0.1 copy.79
  31.4 0.5 reshape.129
  31.9 0.5 copy.56
  32.5 1.2 %convert_element_type.75 = bf16[2,512,2,128]{3,2,1,0:T(2,128)(2,1)S(1)} reshape(bf16[1,1024,256]{2,1,0:T(8,128)(2,1)} %get-tuple-element.12) | data formatting | bytes 1048576 | tf_op jit(solution)/shard_map/convert_element_type | solution.py:65
  33.7 0.1 copy.81
  33.8 0.7 copy.84
  34.5 0.1 fusion.29
  34.6 0.7 copy.83
  35.3 0.6 reshape.137
  35.9 0.1 copy.57
  36.0 0.1 reshape.125
  36.1 1.4 %convolution_convert_fusion.1 = bf16[256,1024]{1,0:T(8,128)(2,1)S(1)} fusion(bf16[256,256]{1,0:T(8,128)(2,1)S(1)} %reshape.125, bf16[256,1024]{1,0:T(8,128)(2,1)} %param.16), kind=kOutput, calls=%fused_computation.29 | convolution fusion | flops 134479872 | bytes 1179648 | tf_op jit(solution)/shard_map/dot_general | solution.py:55
  37.4 0.2 fusion.30
  37.6 0.2 fusion.32
  37.8 1.3 %convolution_convert_fusion.2 = bf16[256,256]{1,0:T(8,128)(2,1)S(1)} fusion(bf16[256,1024]{1,0:T(8,128)(2,1)S(1)} %fusion.32, bf16[4,1024,256]{2,1,0:T(8,128)(2,1)} %param.18), kind=kOutput, calls=%fused_computation.31 | convolution fusion | flops 134283264 | bytes 1179648 | tf_op jit(solution)/shard_map/dot_general | solution.py:121
  39.2 0.1 iota_compare_fusion
  39.3 0.7 fusion.40
  40.1 0.2 copy-done.2
  40.3 5.5 %fusion.20 = f32[2,512,2,128]{1,3,2,0:T(8,128)} fusion(f32[2,2,512,512]{3,2,0,1:T(8,128)S(1)} %fusion.40, f32[2,512]{1,0:T(2,128)} %copy-done.6, f32[2,2,512]{2,0,1:T(2,128)S(1)} %get-tuple-element.14, pred[512,512]{1,0:T(8,128)(4,1)S(1)} %iota_compare_fusion, bf16[2,512,2,128]{3,2,1,0:T(2,128)(2,1)S(1)} %copy-done.2), kind=kOutput, calls=%fused_computation.23 | convolution fusion | flops 1615855616 | bytes 6041600 | tf_op jit(solution)/shard_map/huij,ujhd->uihd/dot_general | solution.py:82
  45.8 3.4 %all-gather.4.cloned.1.call-done = f32[8,2,128,128]{3,2,1,0:T(8,128)} async-done(((f32[2,2,128,128]{3,2,1,0:T(8,128)}), f32[8,2,128,128]{3,2,1,0:T(8,128)}) %all-gather.4.cloned.1.call-update) | async-done | bytes 1048592 | tf_op jit(solution)/shard_map/all_gather | solution.py:97
  49.2 1.5 %multiply_reduce_fusion = (bf16[2,2,128,128]{3,2,1,0:T(8,128)(2,1)S(1)}, f32[2,2,128,128]{3,2,1,0:T(8,128)S(1)}) fusion(f32[2,2,4,128,128]{4,3,1,0,2:T(8,128)} %bitcast.62, f32[2,2,4]{1,0,2:T(2,128)S(1)} %copy-done.4, f32[2,2,4]{1,0,2:T(2,128)S(1)} %copy-done.5), kind=kLoop, calls=%fused_computation.43 | loop fusion | flops 917504 | bytes 1441920
  50.7 0.1 copy.78
  50.8 0.2 multiply_reduce_fusion.3
  51.0 0.8 multiply_multiply_fusion
  51.8 0.2 copy.59
  52.0 2.3 %fusion.54 = f32[256,1024]{1,0:T(8,128)} fusion(bf16[256,1024]{1,0:T(8,128)(2,1)} %param.20, f32[32,8,2,128]{3,2,1,0:T(2,128)S(1)} %bitcast.61, bf16[256,1024]{1,0:T(8,128)(2,1)S(1)} %fusion.32, s32[]{:T(128)S(6)} %select_n.24), kind=kOutput, calls=%fused_computation.72 | convolution fusion | flops 134414336 | bytes 1966084 | tf_op jit(solution)/shard_map/dot_general | solution.py:135
  54.4 0.0 all-reduce.2.cloned.1.call-update
  54.4 2.0 %multiply_reduce_fusion.2 = (f32[2,512,2]{1,2,0:T(2,128)S(1)}, f32[2,512,2,128]{1,3,2,0:T(8,128)S(1)}) fusion(f32[2,512,2,128]{1,3,2,0:T(8,128)} %fusion.20, f32[2,512,2]{1,2,0:T(2,128)S(1)} %get-tuple-element.13, bf16[2,512,2,128]{3,2,1,0:T(2,128)(2,1)S(1)} %convert_element_type.75, f32[2,2,128,128]{3,2,1,0:T(8,128)S(1)} %get-tuple-element.9), kind=kOutput, calls=%fused_computation.46 | convolution fusion | flops 403699712 | bytes 2899968 | tf_op jit(solution)/shard_map/uihd,hude->uihe/dot_general | solution.py:110
  56.4 1.1 %multiply_convert_fusion = bf16[2,512,2,128]{1,3,2,0:T(8,128)(2,1)S(1)} fusion(f32[2,512,2,128]{1,3,2,0:T(8,128)S(1)} %copy.56, f32[2,512,2,128]{1,3,2,0:T(8,128)S(1)} %get-tuple-element.18, f32[2,128]{1,0:T(2,128)} %bitcast.70, f32[2,512,2]{1,2,0:T(2,128)S(1)} %add_rsqrt_fusion), kind=kLoop, calls=%fused_computation.45 | loop fusion | flops 2097152 | bytes 2630656 | tf_op jit(solution)/shard_map/convert_element_type | solution.py:118
  57.4 1.0 %copy.60 = bf16[2,512,256]{2,1,0:T(8,128)(2,1)} copy(bf16[2,512,256]{1,2,0:T(8,128)(2,1)S(1)} %bitcast.60) | data formatting | bytes 1048576
  58.4 31.7 %all-reduce.2.cloned.1.call-done = f32[256,1024]{1,0:T(8,128)} async-done(((f32[256,1024]{1,0:T(8,128)}), f32[256,1024]{1,0:T(8,128)}) %all-reduce.2.cloned.1.call-update) | async-done | bytes 1048592 | tf_op jit(solution)/shard_map/psum | solution.py:134
  90.2 1.2 %convolution_bitcast_fusion.3 = f32[64]{0:T(128)S(1)} fusion(bf16[1024,1]{0,1:T(2,128)(2,1)S(1)} %copy-done.9, f32[256,1024]{1,0:T(8,128)} %all-reduce.2.cloned.1.call-done, s32[]{:T(128)S(6)} %select_n.25), kind=kOutput, calls=%fused_computation.37 | convolution fusion | flops 1048576 | bytes 264452 | tf_op jit(solution)/shard_map/dot_general | solution.py:138
  91.4 0.2 reshape.128
  91.6 0.6 copy.61
  (32 shorter events, 0.2 us)
Async XLA Ops:
  7.2 1.0 %copy-start = (bf16[2,512,256]{2,1,0:T(8,128)(2,1)S(1)}, bf16[2,512,256]{2,1,0:T(8,128)(2,1)}, u32[]{:S(2)}) copy-start(bf16[2,512,256]{2,1,0:T(8,128)(2,1)} %param.11) | copy-start | bytes 1572868
  7.2 3.3 %copy-start.12 = (bf16[4,1024,256]{2,1,0:T(8,128)(2,1)S(1)}, bf16[4,1024,256]{2,1,0:T(8,128)(2,1)}, u32[]{:S(2)}) copy-start(bf16[4,1024,256]{2,1,0:T(8,128)(2,1)} %param.18) | copy-start | bytes 6291460
  7.2 3.3 %copy-start.8 = (f32[1024]{0:T(1024)S(1)}, f32[1024]{0:T(1024)}, u32[]{:S(2)}) copy-start(f32[1024]{0:T(1024)} %param.17) | copy-start | bytes 12292
  7.2 42.0 %all-gather.4.cloned.1.call-start = ((), (), s32[]{:S(2)}) async-start(), calls=%async_computation.1 | async-start | bytes 1310720 | tf_op jit(solution)/shard_map/all_gather | solution.py:97
  12.9 1.2 %copy-start.13 = (s32[2]{0:T(128)S(1)}, s32[2]{0:T(128)}, u32[]{:S(2)}) copy-start(s32[2]{0:T(128)} %param.13) | copy-start | bytes 28
  12.9 1.3 %copy-start.7 = (f32[2,2,512]{2,1,0:T(2,128)S(1)}, f32[2,2,512]{2,1,0:T(2,128)}, u32[]{:S(2)}) copy-start(f32[2,2,512]{2,1,0:T(2,128)} %param.14) | copy-start | bytes 24580
  12.9 3.9 %copy-start.10 = (s32[2,512]{1,0:T(2,128)S(1)}, s32[2,512]{1,0:T(2,128)}, u32[]{:S(2)}) copy-start(s32[2,512]{1,0:T(2,128)} %param.12) | copy-start | bytes 12292
  16.1 15.3 %copy-start.1 = (bf16[2,512,2,128]{3,2,1,0:T(2,128)(2,1)}, bf16[2,512,2,128]{3,2,1,0:T(2,128)(2,1)S(1)}, u32[]{:S(2)}) copy-start(bf16[2,512,2,128]{3,2,1,0:T(2,128)(2,1)S(1)} %convert_element_type.74) | copy-start | bytes 1572868
  16.1 19.1 %copy-start.11 = (bf16[1024]{0:T(1024)(128)(2,1)S(1)}, bf16[1024]{0:T(1024)(128)(2,1)}, u32[]{:S(2)}) copy-start(bf16[1024]{0:T(1024)(128)(2,1)} %param.21) | copy-start | bytes 6148
  16.2 19.7 %copy-start.3 = (bf16[2,128,256]{2,1,0:T(8,128)(2,1)S(1)}, bf16[2,128,256]{2,1,0:T(8,128)(2,1)}, u32[]{:S(2)}) copy-start(bf16[2,128,256]{2,1,0:T(8,128)(2,1)} %param.15) | copy-start | bytes 393220
  16.8 1.5 %copy-start.6 = (f32[2,512]{1,0:T(2,128)}, f32[2,512]{1,0:T(2,128)S(1)}, u32[]{:S(2)}) copy-start(f32[2,512]{1,0:T(2,128)S(1)} %and_convert_fusion) | copy-start | bytes 12292
  18.4 71.8 %all-reduce.2.cloned.1.call-start = ((), (), s32[]{:S(2)}) async-start(), calls=%async_computation | async-start | bytes 2097152 | tf_op jit(solution)/shard_map/psum | solution.py:134
  39.2 1.0 %copy-start.2 = (bf16[2,512,2,128]{3,2,1,0:T(2,128)(2,1)S(1)}, bf16[2,512,2,128]{3,2,1,0:T(2,128)(2,1)}, u32[]{:S(2)}) copy-start(bf16[2,512,2,128]{3,2,1,0:T(2,128)(2,1)} %copy-done.1) | copy-start | bytes 1572868
  40.3 8.9 %copy-start.4 = (f32[2,2,4]{1,0,2:T(2,128)S(1)}, f32[2,2,4]{1,0,2:T(2,128)}, u32[]{:S(2)}) copy-start(f32[2,2,4]{1,0,2:T(2,128)} %copy.84) | copy-start | bytes 196
  40.3 8.9 %copy-start.5 = (f32[2,2,4]{1,0,2:T(2,128)S(1)}, f32[2,2,4]{1,0,2:T(2,128)}, u32[]{:S(2)}) copy-start(f32[2,2,4]{1,0,2:T(2,128)} %copy.83) | copy-start | bytes 196
  54.4 35.8 %copy-start.9 = (bf16[1024,1]{0,1:T(2,128)(2,1)S(1)}, bf16[1024,1]{0,1:T(2,128)(2,1)}, u32[]{:S(2)}) copy-start(bf16[1024,1]{0,1:T(2,128)(2,1)} %reshape.137) | copy-start | bytes 6148
Sparse Core Ops, SparseCore 0:
  18.5 30.6 all-gather.3
  54.5 35.6 all-reduce.1
where the time goes:
time: 99.6 us; the launch traced here: 99 us
  waiting for transfers between devices  35.2 us (35%)
  matrix products  20.2 us (20%)
  between operations  14.4 us (14%)
  blocking collectives  12.8 us (13%)
  local copies, waits for them, and re-layouts  9.09 us (9%)
  other arithmetic  7.31 us (7%)
    psum x1, waiting for transfers between devices, local(): lax.psum(jnp.dot(candidate_feat, ranker_first, preferred_element_type=jnp...  31.7 us
    all_gather x1, blocking collectives, local(): log_rows = lax.all_gather(span_total[None], 'ctx', axis=0, tiled=True)  12.8 us
    dot_general x1, matrix products, local(): jnp.einsum('huij,ujhd->uihd', scores_local * decay_matrix, value_wide, pr...  5.5 us
    unnamed x35, local copies, waits for them, and re-layouts  5.08 us
    all_gather x1, waiting for transfers between devices, local(): shard_piece = lax.all_gather(local_state[None], 'ctx', axis=0, tiled=True)  3.4 us
    dot_general x1, matrix products, local(): jnp.einsum('rd,pdc->prc', behavior_norm, proj_weight, preferred_element_t...  2.39 us
    dot_general x1, matrix products, local(): jnp.dot(candidate_feat, ranker_first, preferred_element_type=jnp.float32)  2.34 us
  transfers between devices with their start and end apart: 2, of which 2 were waited for; matrix products, arithmetic and copies ran while one was open for 18% of the time, Pallas kernels for 0%

commit v1 on v0

v1 whole, which is shorter than its diff:
```python
import functools

import jax
import jax.numpy as jnp
from jax import lax
from jax.experimental import pallas as pl
from jax.experimental.pallas import tpu as pltpu
from jax.sharding import PartitionSpec as P

DH = 128
CORES = 2
EPS = 1e-05
F32 = jnp.float32
BF16 = jnp.bfloat16
MESH = pl.DeviceIdType.MESH


def mm(a, b):
    return jnp.dot(a, b, preferred_element_type=F32)


def mm_tn(a, b):
    return lax.dot_general(a, b, (((0,), (0,)), ((), ())), preferred_element_type=F32)


def mm_nt(a, b):
    return lax.dot_general(a, b, (((1,), (1,)), ((), ())), preferred_element_type=F32)


def silu(x):
    return x / (1.0 + jnp.exp(-x))


def normed(rows, weight, gain):
    raw = mm(rows, weight).astype(BF16).astype(F32)
    scale = lax.rsqrt(jnp.mean(raw * raw, axis=-1, keepdims=True) + EPS)
    return (raw * scale * gain).astype(BF16)


def kernel(
    n_ctx,
    n_head,
    chunk,
    hl,
    be_h,
    mk_h,
    ld_h,
    ce_h,
    iw_h,
    ig_h,
    pw_h,
    og_h,
    rf_h,
    r2_h,
    hist_h,
    score_o,
    be,
    mk,
    ld,
    ce,
    iw,
    ig,
    pw,
    og,
    r2,
    rank,
    norm_s,
    cnorm,
    key_s,
    val_s,
    qry_s,
    gate_s,
    within_s,
    hist,
    dat,
    lst,
    loc,
    tall,
    p_in,
    p_out,
    x_in,
    x_out,
    feat,
    feat_in,
    load_sem,
    out_sem,
    t_send,
    t_recv,
    p_send,
    p_recv,
    x_send,
    x_recv,
    r_send,
    r_recv,
    f_send,
    f_recv,
):
    users, span, _ = be.shape
    cand = ce.shape[1]
    cols = og.shape[1]
    heads = cols // DH
    pairs = heads * users
    chunks = span // chunk
    share = cand // n_head
    me = lax.axis_index("ctx")
    hm = lax.axis_index("head")
    core = lax.rem(hm, CORES)

    loads = {}
    for i, (name, src, dst) in enumerate(
        (
            ("be", be_h, be),
            ("iw", iw_h, iw),
            ("ig", ig_h, ig),
            ("ld", ld_h, ld),
            ("mk", mk_h, mk),
            ("k", pw_h.at[1], pw.at[1]),
            ("v", pw_h.at[2], pw.at[2]),
            ("rf", rf_h, rank.at[hm]),
            ("q", pw_h.at[0], pw.at[0]),
            ("g", pw_h.at[3], pw.at[3]),
            ("og", og_h, og),
            ("ce", ce_h, ce),
            ("r2", r2_h, r2),
        )
    ):
        loads[name] = pltpu.make_async_copy(src, dst, load_sem.at[i])
        loads[name].start()

    barrier = pltpu.get_barrier_semaphore()
    for k in range(1, n_ctx):
        pl.semaphore_signal(
            barrier, inc=1, device_id={"ctx": lax.rem(me + k, n_ctx)}, device_id_type=MESH
        )
    for k in range(1, n_head):
        pl.semaphore_signal(
            barrier, inc=1, device_id={"head": lax.rem(hm + k, n_head)}, device_id_type=MESH
        )

    loads["ld"].wait()
    loads["mk"].wait()
    dat[...] = jnp.zeros_like(dat)
    for h in range(heads):
        dat[h * users : (h + 1) * users, :] = ld[h]
    cum = dat[0:8, :]
    lane = lax.broadcasted_iota(jnp.int32, (8, span), 1)
    in_chunk = lax.rem(lane, chunk)
    step = 1
    while step < chunk:
        cum = cum + jnp.where(in_chunk >= step, pltpu.roll(cum, step, 1), 0.0)
        step *= 2
    ends = [cum[:, (c + 1) * chunk - 1 : (c + 1) * chunk] for c in range(chunks)]
    fades = [jnp.exp(e) for e in ends]
    end_total = functools.reduce(jnp.add, ends)
    fade_total = jnp.exp(end_total)
    end_row = ends[-1]
    for c in range(chunks - 2, -1, -1):
        end_row = jnp.where(lane < (c + 1) * chunk, ends[c], end_row)
    weight_rows = jnp.exp(end_row - cum)
    dat[0:8, :] = cum
    dat[8:16, :] = weight_rows
    dat[16:24, :] = jnp.exp(cum)
    pos = me * span + lax.broadcasted_iota(jnp.int32, (1, span), 1)
    valid = []
    for u in range(users):
        keep = (pos >= n_ctx * span - hl[u]) & (mk[u : u + 1, :] == 1)
        valid.append(jnp.where(keep, 1.0, 0.0))
    for h in range(heads):
        for u in range(users):
            p = 8 + h * users + u
            dat[p : p + 1, :] = dat[p : p + 1, :] * valid[u]
    col = jnp.transpose(dat[...])
    tall[me] = jnp.broadcast_to(end_total, (8, 128))

    pl.semaphore_wait(barrier, n_ctx + n_head - 2)

    t_copies = []
    for k in range(1, n_ctx):
        cp = pltpu.make_async_remote_copy(
            src_ref=tall.at[me],
            dst_ref=tall.at[me],
            send_sem=t_send.at[k],
            recv_sem=t_recv.at[me],
            device_id={"ctx": lax.rem(me + k, n_ctx)},
            device_id_type=MESH,
        )
        cp.start()
        t_copies.append(cp)

    def rank_copy(slot, target, sem):
        return pltpu.make_async_remote_copy(
            src_ref=rank.at[slot],
            dst_ref=rank.at[slot],
            send_sem=r_send.at[sem],
            recv_sem=r_recv.at[slot],
            device_id={"head": target},
            device_id_type=MESH,
        )

    sibling = hm + 1 - 2 * core
    loads["rf"].wait()
    rank_copies = []
    for k in range(CORES, n_head, CORES):
        rank_copies.append(rank_copy(hm, lax.rem(hm + k, n_head), k))
        rank_copies[-1].start()
    rank_copies.append(rank_copy(hm, sibling, 0))
    rank_copies[-1].start()

    loads["be"].wait()
    loads["iw"].wait()
    loads["ig"].wait()
    loads["k"].wait()
    loads["v"].wait()
    weight = iw[...]
    gain = ig[...]
    blocks = [(u, c) for u in range(users) for c in range(chunks)]
    for b, (u, c) in enumerate(blocks):
        r = slice(b * chunk, (b + 1) * chunk)
        rc = slice(c * chunk, (c + 1) * chunk)
        rows = normed(be[u, rc, :], weight, gain)
        norm_s[r, :] = rows
        key = (mm(rows, pw[1]) * DH ** (-0.5)).astype(BF16)
        val = mm(rows, pw[2]).astype(BF16)
        key_s[r, :] = key
        val_s[r, :] = val
        for h in range(heads):
            p = h * users + u
            hc = slice(h * DH, (h + 1) * DH)
            kw = (key[:, hc].astype(F32) * col[rc, 8 + p : 9 + p]).astype(BF16)
            lst[p, c] = mm_tn(kw, val[:, hc])
    for p in range(pairs):
        total = lst[p, 0]
        for c in range(1, chunks):
            total = total * fades[c][p : p + 1, :] + lst[p, c]
        loc[p] = total

    def right_copy(p):
        return pltpu.make_async_remote_copy(
            src_ref=p_out.at[p],
            dst_ref=p_in.at[p],
            send_sem=p_send.at[p],
            recv_sem=p_recv.at[p],
            device_id={"ctx": lax.rem(me + 1, n_ctx)},
            device_id_type=MESH,
        )

    def left_copy(p):
        return pltpu.make_async_remote_copy(
            src_ref=x_out.at[p],
            dst_ref=x_in.at[p],
            send_sem=x_send.at[p],
            recv_sem=x_recv.at[p],
            device_id={"ctx": lax.rem(me + n_ctx - 1, n_ctx)},
            device_id_type=MESH,
        )

    last = n_ctx - 1

    @pl.when(me == 0)
    def _():
        p_in[...] = jnp.zeros_like(p_in)
        for p in range(pairs):
            p_out[p] = loc[p].astype(p_out.dtype)
            if n_ctx > 1:
                right_copy(p).start()

    @pl.when(me == last)
    def _():
        x_in[...] = jnp.zeros_like(x_in)
        for p in range(pairs):
            x_out[p] = loc[p].astype(x_out.dtype)
            if n_ctx > 1:
                left_copy(p).start()

    loads["q"].wait()
    loads["g"].wait()
    loads["og"].wait()
    out_gain = og[...]
    for b in range(len(blocks)):
        r = slice(b * chunk, (b + 1) * chunk)
        rows = norm_s[r, :]
        qry_s[r, :] = mm(rows, pw[0]).astype(BF16)
        gate_s[r, :] = silu(mm(rows, pw[3]).astype(BF16).astype(F32)) * out_gain

    for k in range(1, n_ctx):
        src = lax.rem(me + n_ctx - k, n_ctx)
        pltpu.make_async_remote_copy(
            src_ref=tall.at[src],
            dst_ref=tall.at[src],
            send_sem=t_send.at[k],
            recv_sem=t_recv.at[src],
            device_id={"ctx": lax.rem(me + k, n_ctx)},
            device_id_type=MESH,
        ).wait_recv()
    after = jnp.zeros((8, 128), F32)
    for j in range(n_ctx):
        after = after + jnp.where(j > me, tall[j], 0.0)
    fade_after = jnp.exp(after)[:, 0:1]

    def relay_right():
        for p in range(pairs):
            right_copy(p).wait_recv()

            @pl.when(me < last)
            def _():
                p_out[p] = (
                    p_in[p].astype(F32) * fade_total[p : p + 1, :] + loc[p]
                ).astype(p_out.dtype)
                right_copy(p).start()

    def relay_left():
        for p in range(pairs):
            left_copy(p).wait_recv()

            @pl.when(me > 0)
            def _():
                x_out[p] = (
                    x_in[p].astype(F32) + loc[p] * fade_after[p : p + 1, :]
                ).astype(x_out.dtype)
                left_copy(p).start()

    half = n_ctx // 2
    if n_ctx > 1:

        @pl.when((me > 0) & (me < half))
        def _():
            relay_right()

        @pl.when((me < last) & (me >= half))
        def _():
            relay_left()

    tri = lax.broadcasted_iota(jnp.int32, (chunk, chunk), 0) >= lax.broadcasted_iota(
        jnp.int32, (chunk, chunk), 1
    )
    for b, (u, c) in enumerate(blocks):
        r = slice(b * chunk, (b + 1) * chunk)
        rc = slice(c * chunk, (c + 1) * chunk)
        seen = tri & (valid[u][:, rc] > 0.5)
        for h in range(heads):
            p = h * users + u
            hc = slice(h * DH, (h + 1) * DH)
            gap = col[rc, p : p + 1] - dat[p : p + 1, rc]
            decay = jnp.where(seen, jnp.exp(jnp.where(tri, gap, 0.0)), 0.0)
            att = (mm_nt(qry_s[r, hc], key_s[r, hc]) * decay).astype(BF16)
            within_s[r, hc] = mm(att, val_s[r, hc])

    loads["ce"].wait()
    loads["r2"].wait()
    cnorm[...] = normed(ce[...].reshape(users * cand, ce.shape[2]), weight, gain)
    cand_q = mm(cnorm[...], pw[0]).astype(BF16)
    own = cnorm[:, pl.ds(pl.multiple_of(hm * cols, DH), cols)].astype(F32)

    if n_ctx > 1:

        @pl.when((me < last) & (me < half))
        def _():
            relay_left()

        @pl.when((me > 0) & (me >= half))
        def _():
            relay_right()

    for p in range(pairs):
        h, u = p // users, p % users
        hc = slice(h * DH, (h + 1) * DH)
        rows = slice(u * cand, (u + 1) * cand)
        state = p_in[p].astype(F32) * fade_total[p : p + 1, :] + loc[p]
        state = state * fade_after[p : p + 1, :] + x_in[p].astype(F32)
        read = mm(cand_q[rows, hc], state.astype(BF16))
        scale = lax.rsqrt(jnp.mean(read * read, axis=-1, keepdims=True) + EPS)
        feat[u, :, hc] = (read * scale * out_gain[:, hc] + own[rows, hc]).astype(BF16)

    def feat_copy(k):
        target = lax.rem(hm + k, n_head)
        return pltpu.make_async_remote_copy(
            src_ref=feat.at[:, pl.ds(pl.multiple_of(target * share, share), share), :],
            dst_ref=feat_in.at[hm],
            send_sem=f_send.at[k],
            recv_sem=f_recv.at[hm],
            device_id={"head": target},
            device_id_type=MESH,
        )

    for k in range(1, n_head):
        feat_copy(k).start()

    for k in range(CORES, n_head, CORES):
        src = lax.rem(hm + n_head - k, n_head)
        rank_copy(src, sibling, k).wait_recv()
        rank_copies.append(rank_copy(src, sibling, n_head + k))
        rank_copies[-1].start()

    out_copies = []
    for u in range(users):
        for h in range(heads):
            p = h * users + u
            hc = slice(h * DH, (h + 1) * DH)
            state = p_in[p].astype(F32)
            for c in range(chunks):
                r = slice((u * chunks + c) * chunk, (u * chunks + c + 1) * chunk)
                rc = slice(c * chunk, (c + 1) * chunk)
                read = within_s[r, hc] + col[rc, 16 + p : 17 + p] * mm(
                    qry_s[r, hc], state.astype(BF16)
                )
                scale = lax.rsqrt(jnp.mean(read * read, axis=-1, keepdims=True) + EPS)
                hist[u, rc, hc] = (read * scale * gate_s[r, hc]).astype(BF16)
                if c + 1 < chunks:
                    state = state * fades[c][p : p + 1, :] + lst[p, c]
        out_copies.append(pltpu.make_async_copy(hist.at[u], hist_h.at[u], out_sem.at[u]))
        out_copies[-1].start()

    mine = feat[:, pl.ds(pl.multiple_of(hm * share, share), share), :]
    hidden = mm(mine.reshape(users * share, cols), rank[hm])
    rank_copy(sibling, sibling, 0).wait_recv()
    for k in range(CORES, n_head, CORES):
        src = lax.rem(sibling + n_head - k, n_head)
        rank_copy(src, sibling, n_head + k).wait_recv()
    for k in range(1, n_head):
        src = lax.rem(hm + n_head - k, n_head)
        pltpu.make_async_remote_copy(
            src_ref=feat_in.at[src],
            dst_ref=feat_in.at[src],
            send_sem=f_send.at[k],
            recv_sem=f_recv.at[src],
            device_id={"head": src},
            device_id_type=MESH,
        ).wait_recv()
        hidden = hidden + mm(feat_in[src].reshape(users * share, cols), rank[src])
    acted = silu(hidden) * r2[...].astype(F32)
    score_o[...] = jnp.sum(acted.reshape(users, share, acted.shape[1]), axis=-1)

    for cp in t_copies + rank_copies:
        cp.wait_send()
    for k in range(1, n_head):
        feat_copy(k).wait_send()
    if n_ctx > 1:

        @pl.when(me < last)
        def _():
            for p in range(pairs):
                right_copy(p).wait_send()

        @pl.when(me > 0)
        def _():
            for p in range(pairs):
                left_copy(p).wait_send()

    for cp in out_copies:
        cp.wait()


def local(
    n_ctx,
    n_head,
    behavior_embed,
    behavior_mask,
    history_len,
    log_decay,
    candidate_embed,
    input_weight,
    input_gain,
    proj_weight,
    output_gain,
    ranker_first,
    ranker_second,
):
    users, span, embed = behavior_embed.shape
    cand = candidate_embed.shape[1]
    width, cols = proj_weight.shape[1:]
    hidden = ranker_first.shape[1]
    heads = cols // DH
    pairs = heads * users
    chunk = 256 if span % 256 == 0 else 128
    chunks = span // chunk
    share = cand // n_head
    wire = BF16 if n_ctx <= 8 else F32
    rows = users * span
    dma = pltpu.SemaphoreType.DMA
    any_spec = pl.BlockSpec(memory_space=pl.ANY)
    flops = 2 * rows * width * (embed + 4 * cols)
    history_out, scores = pl.pallas_call(
        functools.partial(kernel, n_ctx, n_head, chunk),
        out_shape=(
            jax.ShapeDtypeStruct((users, span, cols), BF16),
            jax.ShapeDtypeStruct((users, share), F32),
        ),
        in_specs=[pl.BlockSpec(memory_space=pltpu.SMEM)] + [any_spec] * 10,
        out_specs=(any_spec, pl.BlockSpec(memory_space=pltpu.VMEM)),
        scratch_shapes=[
            pltpu.VMEM((users, span, embed), BF16),
            pltpu.VMEM((users, span), jnp.int32),
            pltpu.VMEM((heads, users, span), F32),
            pltpu.VMEM((users, cand, embed), BF16),
            pltpu.VMEM((embed, width), BF16),
            pltpu.VMEM((1, width), F32),
            pltpu.VMEM((4, width, cols), BF16),
            pltpu.VMEM((1, cols), F32),
            pltpu.VMEM((1, hidden), BF16),
            pltpu.VMEM((n_head, cols, hidden), BF16),
            pltpu.VMEM((rows, width), BF16),
            pltpu.VMEM((users * cand, width), BF16),
            pltpu.VMEM((rows, cols), BF16),
            pltpu.VMEM((rows, cols), BF16),
            pltpu.VMEM((rows, cols), BF16),
            pltpu.VMEM((rows, cols), F32),
            pltpu.VMEM((rows, cols), F32),
            pltpu.VMEM((users, span, cols), BF16),
            pltpu.VMEM((24, span), F32),
            pltpu.VMEM((pairs, chunks, DH, DH), F32),
            pltpu.VMEM((pairs, DH, DH), F32),
            pltpu.VMEM((n_ctx, 8, 128), F32),
            pltpu.VMEM((pairs, DH, DH), wire),
            pltpu.VMEM((pairs, DH, DH), wire),
            pltpu.VMEM((pairs, DH, DH), wire),
            pltpu.VMEM((pairs, DH, DH), wire),
            pltpu.VMEM((users, cand, cols), BF16),
            pltpu.VMEM((n_head, users, share, cols), BF16),
            dma((13,)),
            dma((users,)),
            dma((n_ctx,)),
            dma((n_ctx,)),
            dma((pairs,)),
            dma((pairs,)),
            dma((pairs,)),
            dma((pairs,)),
            dma((2 * n_head,)),
            dma((n_head,)),
            dma((n_head,)),
            dma((n_head,)),
        ],
        compiler_params=pltpu.CompilerParams(
            collective_id=0, has_side_effects=True, vmem_limit_bytes=48 * 1024 * 1024
        ),
        cost_estimate=pl.CostEstimate(
            flops=flops, bytes_accessed=6 * 1024 * 1024, transcendentals=0
        ),
    )(
        history_len,
        behavior_embed,
        behavior_mask,
        log_decay,
        candidate_embed,
        input_weight,
        input_gain.reshape(1, width),
        proj_weight,
        output_gain.reshape(1, cols),
        ranker_first,
        ranker_second.reshape(1, hidden),
    )
    return history_out, scores


def solution(mesh):
    in_specs = (
        P("grp", "ctx", None),
        P("grp", "ctx"),
        P("grp"),
        P("head", "grp", "ctx"),
        P("grp", "ctx", None),
        P(),
        P(),
        P(None, None, "head"),
        P("head"),
        P("head", None),
        P(),
    )
    out_specs = (P("grp", "ctx", "head"), P("grp", ("ctx", "head")))
    return jax.shard_map(
        functools.partial(local, mesh.shape["ctx"], mesh.shape["head"]),
        mesh=mesh,
        in_specs=in_specs,
        out_specs=out_specs,
        check_vma=False,
    )
```

time: 99.6 us -> 36.9 us (0.37)
  waiting for transfers between devices: 35.2 us -> 0 us
  Pallas kernels: 0 us -> 24.7 us
  matrix products: 20.2 us -> 0 us
  between operations: 14.4 us -> 0.65 us
  blocking collectives: 12.8 us -> 0 us
  other arithmetic: 7.31 us -> 0 us
  local copies, waits for them, and re-layouts: 9.09 us -> 11.1 us
    psum x1 -> x0, waiting for transfers between devices: 31.7 us -> none  [local(): lax.psum(jnp.dot(candidate_feat, ranker_first, preferred_element_type=jnp...]
    pallas_call x0 -> x1, Pallas kernels: none -> 24.7 us  [local(): pl.pallas_call(functools.partial(kernel, n_ctx, n_head, chunk), out_shape...]
    dot_general x11 -> x0, matrix products: 20.2 us -> none  [the longest x1 5.5 us: local(): jnp.einsum('huij,ujhd->uihd', scores_local * decay_matrix, value_wide, pr...]
    all_gather x1 -> x0, blocking collectives: 12.8 us -> none  [local(): log_rows = lax.all_gather(span_total[None], 'ctx', axis=0, tiled=True)]
    unnamed x35 -> x22, local copies, waits for them, and re-layouts: 5.08 us -> 10.4 us
    all_gather x1 -> x0, waiting for transfers between devices: 3.4 us -> none  [local(): shard_piece = lax.all_gather(local_state[None], 'ctx', axis=0, tiled=True)]
    convert_element_type x6 -> x0, local copies, waits for them, and re-layouts: 2.9 us -> none  [the longest x1 1.17 us: local(): query_rows = projected[0].astype(jnp.bfloat16).reshape(head_shape)]
    another operation x4 -> x0, other arithmetic: 1.69 us -> none
  transfers between devices with their start and end apart: 2 -> 0, of which waited for: 2 -> 0; matrix products, arithmetic and copies ran while one was open for 18% -> 0% of each run, Pallas kernels for 0% -> 0%
where the time goes in v1:
time: 36.9 us; the launch traced here: 36.4 us
  Pallas kernels  24.7 us (67%)
  local copies, waits for them, and re-layouts  11.1 us (30%)
  between operations  0.65 us (2%)
    pallas_call x1, Pallas kernels, local(): pl.pallas_call(functools.partial(kernel, n_ctx, n_head, chunk), out_shape...  24.7 us
    unnamed x22, local copies, waits for them, and re-layouts  10.4 us

profile of v1, /device:TPU:0, one launch (start us, length us, event | category | flops | bytes accessed | tf_op | source)
XLA Modules:
  0.0 36.4 jit_solution(12236705755869410257)
XLA Ops:
  0.6 0.7 %reshape.15.r2_h = bf16[1,1024]{1,0:T(2,128)(2,1)S(1)} reshape(bf16[1024]{0:T(1024)(128)(2,1)} %param.21) | data formatting | bytes 4096 | tf_op jit(solution)/shard_map/reshape | solution.py:549
  1.3 0.0 copy-start
  1.3 1.6 %copy-done = bf16[4,1024,256]{2,1,0:T(8,128)(2,1)S(1)} copy-done((bf16[4,1024,256]{2,1,0:T(8,128)(2,1)S(1)}, bf16[4,1024,256]{2,1,0:T(8,128)(2,1)}, u32[]{:S(2)}) %copy-start) | copy-done | bytes 2097176
  2.9 0.0 copy-start.1
  2.9 1.0 %copy-done.1 = bf16[2,512,256]{2,1,0:T(8,128)(2,1)S(1)} copy-done((bf16[2,512,256]{2,1,0:T(8,128)(2,1)S(1)}, bf16[2,512,256]{2,1,0:T(8,128)(2,1)}, u32[]{:S(2)}) %copy-start.1) | copy-done | bytes 524312
  4.0 0.0 copy-start.2
  4.0 1.0 %copy-done.2 = bf16[256,1024]{1,0:T(8,128)(2,1)S(1)} copy-done((bf16[256,1024]{1,0:T(8,128)(2,1)S(1)}, bf16[256,1024]{1,0:T(8,128)(2,1)}, u32[]{:S(2)}) %copy-start.2) | copy-done | bytes 524312
  5.0 0.0 copy-start.3
  5.0 1.0 %copy-done.3 = bf16[256,1024]{1,0:T(8,128)(2,1)S(1)} copy-done((bf16[256,1024]{1,0:T(8,128)(2,1)S(1)}, bf16[256,1024]{1,0:T(8,128)(2,1)}, u32[]{:S(2)}) %copy-start.3) | copy-done | bytes 524312
  6.0 0.0 copy-start.4
  6.0 0.9 %copy-done.4 = bf16[2,128,256]{2,1,0:T(8,128)(2,1)S(1)} copy-done((bf16[2,128,256]{2,1,0:T(8,128)(2,1)S(1)}, bf16[2,128,256]{2,1,0:T(8,128)(2,1)}, u32[]{:S(2)}) %copy-start.4) | copy-done | bytes 131096
  6.9 0.0 copy-start.5
  6.9 0.7 %copy-done.5 = f32[2,2,512]{2,1,0:T(2,128)S(1)} copy-done((f32[2,2,512]{2,1,0:T(2,128)S(1)}, f32[2,2,512]{2,1,0:T(2,128)}, u32[]{:S(2)}) %copy-start.5) | copy-done | bytes 8216
  7.6 0.0 copy-start.6
  7.6 0.7 %copy-done.6 = s32[2,512]{1,0:T(2,128)S(1)} copy-done((s32[2,512]{1,0:T(2,128)S(1)}, s32[2,512]{1,0:T(2,128)}, u32[]{:S(2)}) %copy-start.6) | copy-done | bytes 4120
  8.3 0.0 copy-start.7
  8.3 0.7 %copy-done.7 = f32[1024]{0:T(1024)S(1)} copy-done((f32[1024]{0:T(1024)S(1)}, f32[1024]{0:T(1024)}, u32[]{:S(2)}) %copy-start.7) | copy-done | bytes 4120
  9.0 0.0 copy-start.8
  9.0 0.7 %copy-done.8 = f32[256]{0:T(256)S(1)} copy-done((f32[256]{0:T(256)S(1)}, f32[256]{0:T(256)}, u32[]{:S(2)}) %copy-start.8) | copy-done | bytes 1048
  9.7 0.0 copy-start.9
  9.7 0.7 %copy-done.9 = s32[2]{0:T(128)S(1)} copy-done((s32[2]{0:T(128)S(1)}, s32[2]{0:T(128)}, u32[]{:S(2)}) %copy-start.9) | copy-done | bytes 32
  10.3 24.7 %shard_map.122 = (bf16[2,512,256]{2,1,0:T(8,128)(2,1)S(1)}, f32[2,32]{1,0:T(2,128)S(1)}) custom-call(s32[2]{0:T(128)S(1)} %copy-done.9, bf16[2,512,256]{2,1,0:T(8,128)(2,1)S(1)} %copy-done.1, s32[2,512]{1,0:T(2,128)S(1)} %copy-done.6, f32[2,2,512]{2,1,0:T(2,128)S(1)} %copy-done.5, bf16[2,128,256]{2,1,0:T(8,128)(2,1)S(1)} %copy-done.4, ...), custom_call_target="tpu_custom_call" | custom-call | flops 2684354560 | bytes 6291456 | tf_op jit(solution)/shard_map/pallas_call | solution.py:482
  35.1 0.8 %copy.15 = bf16[2,512,256]{2,1,0:T(8,128)(2,1)} copy(bf16[2,512,256]{2,1,0:T(8,128)(2,1)S(1)} %get-tuple-element.4) | data formatting | bytes 1048576
  35.9 0.6 %copy.16 = f32[2,32]{1,0:T(2,128)} copy(f32[2,32]{1,0:T(2,128)S(1)} %get-tuple-element.5) | data formatting | bytes 512
Async XLA Ops:
  1.3 1.6 %copy-start = (bf16[4,1024,256]{2,1,0:T(8,128)(2,1)S(1)}, bf16[4,1024,256]{2,1,0:T(8,128)(2,1)}, u32[]{:S(2)}) copy-start(bf16[4,1024,256]{2,1,0:T(8,128)(2,1)} %pw_h.1) | copy-start | bytes 6291460
  2.9 1.0 %copy-start.1 = (bf16[2,512,256]{2,1,0:T(8,128)(2,1)S(1)}, bf16[2,512,256]{2,1,0:T(8,128)(2,1)}, u32[]{:S(2)}) copy-start(bf16[2,512,256]{2,1,0:T(8,128)(2,1)} %be_h.1) | copy-start | bytes 1572868
  4.0 1.0 %copy-start.2 = (bf16[256,1024]{1,0:T(8,128)(2,1)S(1)}, bf16[256,1024]{1,0:T(8,128)(2,1)}, u32[]{:S(2)}) copy-start(bf16[256,1024]{1,0:T(8,128)(2,1)} %iw_h.1) | copy-start | bytes 1572868
  5.0 1.0 %copy-start.3 = (bf16[256,1024]{1,0:T(8,128)(2,1)S(1)}, bf16[256,1024]{1,0:T(8,128)(2,1)}, u32[]{:S(2)}) copy-start(bf16[256,1024]{1,0:T(8,128)(2,1)} %rf_h.1) | copy-start | bytes 1572868
  6.0 0.9 %copy-start.4 = (bf16[2,128,256]{2,1,0:T(8,128)(2,1)S(1)}, bf16[2,128,256]{2,1,0:T(8,128)(2,1)}, u32[]{:S(2)}) copy-start(bf16[2,128,256]{2,1,0:T(8,128)(2,1)} %ce_h.1) | copy-start | bytes 393220
  6.9 0.7 %copy-start.5 = (f32[2,2,512]{2,1,0:T(2,128)S(1)}, f32[2,2,512]{2,1,0:T(2,128)}, u32[]{:S(2)}) copy-start(f32[2,2,512]{2,1,0:T(2,128)} %ld_h.1) | copy-start | bytes 24580
  7.6 0.7 %copy-start.6 = (s32[2,512]{1,0:T(2,128)S(1)}, s32[2,512]{1,0:T(2,128)}, u32[]{:S(2)}) copy-start(s32[2,512]{1,0:T(2,128)} %mk_h.1) | copy-start | bytes 12292
  8.3 0.7 %copy-start.7 = (f32[1024]{0:T(1024)S(1)}, f32[1024]{0:T(1024)}, u32[]{:S(2)}) copy-start(f32[1024]{0:T(1024)} %param.17) | copy-start | bytes 12292
  9.0 0.7 %copy-start.8 = (f32[256]{0:T(256)S(1)}, f32[256]{0:T(256)}, u32[]{:S(2)}) copy-start(f32[256]{0:T(256)} %param.19) | copy-start | bytes 3076
  9.7 0.7 %copy-start.9 = (s32[2]{0:T(128)S(1)}, s32[2]{0:T(128)}, u32[]{:S(2)}) copy-start(s32[2]{0:T(128)} %hl.1) | copy-start | bytes 28

commit v2 on v1

--- a/solution.py
+++ b/solution.py
@@ -109,6 +109,7 @@
     loads = {}
     for i, (name, src, dst) in enumerate(
         (
+            ("rf", rf_h, rank.at[hm]),
             ("be", be_h, be),
             ("iw", iw_h, iw),
             ("ig", ig_h, ig),
@@ -116,7 +117,6 @@
             ("mk", mk_h, mk),
             ("k", pw_h.at[1], pw.at[1]),
             ("v", pw_h.at[2], pw.at[2]),
-            ("rf", rf_h, rank.at[hm]),
             ("q", pw_h.at[0], pw.at[0]),
             ("g", pw_h.at[3], pw.at[3]),
             ("og", og_h, og),
@@ -137,11 +137,34 @@
             barrier, inc=1, device_id={"head": lax.rem(hm + k, n_head)}, device_id_type=MESH
         )
 
+    pl.semaphore_wait(barrier, n_ctx + n_head - 2)
+
+    def rank_copy(slot, target, sem):
+        return pltpu.make_async_remote_copy(
+            src_ref=rank.at[slot],
+            dst_ref=rank.at[slot],
+            send_sem=r_send.at[sem],
+            recv_sem=r_recv.at[slot],
+            device_id={"head": target},
+            device_id_type=MESH,
+        )
+
+    sibling = hm + 1 - 2 * core
+    loads["rf"].wait()
+    rank_copies = []
+    for k in range(CORES, n_head, CORES):
+        rank_copies.append(rank_copy(hm, lax.rem(hm + k, n_head), k))
+        rank_copies[-1].start()
+    rank_copies.append(rank_copy(hm, sibling, 0))
+    rank_copies[-1].start()
+
     loads["ld"].wait()
     loads["mk"].wait()
     dat[...] = jnp.zeros_like(dat)
-    for h in range(heads):
-        dat[h * users : (h + 1) * users, :] = ld[h]
+    for u in range(users):
+        for h in range(heads):
+            p = u * heads + h
+            dat[p : p + 1, :] = ld[h, u : u + 1, :]
     cum = dat[0:8, :]
     lane = lax.broadcasted_iota(jnp.int32, (8, span), 1)
     in_chunk = lax.rem(lane, chunk)
@@ -167,12 +190,10 @@
         valid.append(jnp.where(keep, 1.0, 0.0))
     for h in range(heads):
         for u in range(users):
-            p = 8 + h * users + u
+            p = 8 + u * heads + h
             dat[p : p + 1, :] = dat[p : p + 1, :] * valid[u]
     col = jnp.transpose(dat[...])
     tall[me] = jnp.broadcast_to(end_total, (8, 128))
-
-    pl.semaphore_wait(barrier, n_ctx + n_head - 2)
 
     t_copies = []
     for k in range(1, n_ctx):
@@ -187,24 +208,35 @@
         cp.start()
         t_copies.append(cp)
 
-    def rank_copy(slot, target, sem):
+    def right_copy(p):
         return pltpu.make_async_remote_copy(
-            src_ref=rank.at[slot],
-            dst_ref=rank.at[slot],
-            send_sem=r_send.at[sem],
-            recv_sem=r_recv.at[slot],
-            device_id={"head": target},
-            device_id_type=MESH,
-        )
-
-    sibling = hm + 1 - 2 * core
-    loads["rf"].wait()
-    rank_copies = []
-    for k in range(CORES, n_head, CORES):
-        rank_copies.append(rank_copy(hm, lax.rem(hm + k, n_head), k))
-        rank_copies[-1].start()
-    rank_copies.append(rank_copy(hm, sibling, 0))
-    rank_copies[-1].start()
+            src_ref=p_out.at[p],
+            dst_ref=p_in.at[p],
+            send_sem=p_send.at[p],
+            recv_sem=p_recv.at[p],
+            device_id={"ctx": lax.rem(me + 1, n_ctx)},
+            device_id_type=MESH,
+        )
+
+    def left_copy(p):
+        return pltpu.make_async_remote_copy(
+            src_ref=x_out.at[p],
+            dst_ref=x_in.at[p],
+            send_sem=x_send.at[p],
+            recv_sem=x_recv.at[p],
+            device_id={"ctx": lax.rem(me + n_ctx - 1, n_ctx)},
+            device_id_type=MESH,
+        )
+
+    last = n_ctx - 1
+
+    @pl.when(me == 0)
+    def _():
+        p_in[...] = jnp.zeros_like(p_in)
+
+    @pl.when(me == last)
+    def _():
+        x_in[...] = jnp.zeros_like(x_in)
 
     loads["be"].wait()
     loads["iw"].wait()
@@ -214,63 +246,42 @@
     weight = iw[...]
     gain = ig[...]
     blocks = [(u, c) for u in range(users) for c in range(chunks)]
-    for b, (u, c) in enumerate(blocks):
-        r = slice(b * chunk, (b + 1) * chunk)
-        rc = slice(c * chunk, (c + 1) * chunk)
-        rows = normed(be[u, rc, :], weight, gain)
-        norm_s[r, :] = rows
-        key = (mm(rows, pw[1]) * DH ** (-0.5)).astype(BF16)
-        val = mm(rows, pw[2]).astype(BF16)
-        key_s[r, :] = key
-        val_s[r, :] = val
-        for h in range(heads):
-            p = h * users + u
-            hc = slice(h * DH, (h + 1) * DH)
-            kw = (key[:, hc].astype(F32) * col[rc, 8 + p : 9 + p]).astype(BF16)
-            lst[p, c] = mm_tn(kw, val[:, hc])
-    for p in range(pairs):
-        total = lst[p, 0]
-        for c in range(1, chunks):
-            total = total * fades[c][p : p + 1, :] + lst[p, c]
-        loc[p] = total
-
-    def right_copy(p):
-        return pltpu.make_async_remote_copy(
-            src_ref=p_out.at[p],
-            dst_ref=p_in.at[p],
-            send_sem=p_send.at[p],
-            recv_sem=p_recv.at[p],
-            device_id={"ctx": lax.rem(me + 1, n_ctx)},
-            device_id_type=MESH,
-        )
-
-    def left_copy(p):
-        return pltpu.make_async_remote_copy(
-            src_ref=x_out.at[p],
-            dst_ref=x_in.at[p],
-            send_sem=x_send.at[p],
-            recv_sem=x_recv.at[p],
-            device_id={"ctx": lax.rem(me + n_ctx - 1, n_ctx)},
-            device_id_type=MESH,
-        )
-
-    last = n_ctx - 1
-
-    @pl.when(me == 0)
-    def _():
-        p_in[...] = jnp.zeros_like(p_in)
-        for p in range(pairs):
-            p_out[p] = loc[p].astype(p_out.dtype)
-            if n_ctx > 1:
-                right_copy(p).start()
-
-    @pl.when(me == last)
-    def _():
-        x_in[...] = jnp.zeros_like(x_in)
-        for p in range(pairs):
-            x_out[p] = loc[p].astype(x_out.dtype)
-            if n_ctx > 1:
-                left_copy(p).start()
+    for u in range(users):
+        for c in range(chunks):
+            b = u * chunks + c
+            r = slice(b * chunk, (b + 1) * chunk)
+            rc = slice(c * chunk, (c + 1) * chunk)
+            rows = normed(be[u, rc, :], weight, gain)
+            norm_s[r, :] = rows
+            key = (mm(rows, pw[1]) * DH ** (-0.5)).astype(BF16)
+            val = mm(rows, pw[2]).astype(BF16)
+            key_s[r, :] = key
+            val_s[r, :] = val
+            for h in range(heads):
+                p = u * heads + h
+                hc = slice(h * DH, (h + 1) * DH)
+                kw = (key[:, hc].astype(F32) * col[rc, 8 + p : 9 + p]).astype(BF16)
+                lst[p, c] = mm_tn(kw, val[:, hc])
+        mine = range(u * heads, (u + 1) * heads)
+        for p in mine:
+            total = lst[p, 0]
+            for c in range(1, chunks):
+                total = total * fades[c][p : p + 1, :] + lst[p, c]
+            loc[p] = total
+
+        @pl.when(me == 0)
+        def _():
+            for p in mine:
+                p_out[p] = loc[p].astype(p_out.dtype)
+                if n_ctx > 1:
+                    right_copy(p).start()
+
+        @pl.when(me == last)
+        def _():
+            for p in mine:
+                x_out[p] = loc[p].astype(x_out.dtype)
+                if n_ctx > 1:
+                    left_copy(p).start()
 
     loads["q"].wait()
     loads["g"].wait()
@@ -338,7 +349,7 @@
         rc = slice(c * chunk, (c + 1) * chunk)
         seen = tri & (valid[u][:, rc] > 0.5)
         for h in range(heads):
-            p = h * users + u
+            p = u * heads + h
             hc = slice(h * DH, (h + 1) * DH)
             gap = col[rc, p : p + 1] - dat[p : p + 1, rc]
             decay = jnp.where(seen, jnp.exp(jnp.where(tri, gap, 0.0)), 0.0)
@@ -362,7 +373,7 @@
             relay_right()
 
     for p in range(pairs):
-        h, u = p // users, p % users
+        u, h = p // heads, p % heads
         hc = slice(h * DH, (h + 1) * DH)
         rows = slice(u * cand, (u + 1) * cand)
         state = p_in[p].astype(F32) * fade_total[p : p + 1, :] + loc[p]
@@ -394,7 +405,7 @@
     out_copies = []
     for u in range(users):
         for h in range(heads):
-            p = h * users + u
+            p = u * heads + h
             hc = slice(h * DH, (h + 1) * DH)
             state = p_in[p].astype(F32)
             for c in range(chunks):
@@ -427,8 +438,12 @@
             device_id_type=MESH,
         ).wait_recv()
         hidden = hidden + mm(feat_in[src].reshape(users * share, cols), rank[src])
-    acted = silu(hidden) * r2[...].astype(F32)
-    score_o[...] = jnp.sum(acted.reshape(users, share, acted.shape[1]), axis=-1)
+    second = r2[...].astype(F32)
+    acted = silu(hidden)
+    summed = acted[:, 0:128] * second[0:1, :]
+    for i in range(1, second.shape[0]):
+        summed = summed + acted[:, i * 128 : (i + 1) * 128] * second[i : i + 1, :]
+    score_o[...] = jnp.sum(summed.reshape(users, share, 128), axis=-1)
 
     for cp in t_copies + rank_copies:
         cp.wait_send()
@@ -477,7 +492,8 @@
     wire = BF16 if n_ctx <= 8 else F32
     rows = users * span
     dma = pltpu.SemaphoreType.DMA
-    any_spec = pl.BlockSpec(memory_space=pl.ANY)
+    hbm_spec = pl.BlockSpec(memory_space=pltpu.HBM)
+    vmem_spec = pl.BlockSpec(memory_space=pltpu.VMEM)
     flops = 2 * rows * width * (embed + 4 * cols)
     history_out, scores = pl.pallas_call(
         functools.partial(kernel, n_ctx, n_head, chunk),
@@ -485,8 +501,8 @@
             jax.ShapeDtypeStruct((users, span, cols), BF16),
             jax.ShapeDtypeStruct((users, share), F32),
         ),
-        in_specs=[pl.BlockSpec(memory_space=pltpu.SMEM)] + [any_spec] * 10,
-        out_specs=(any_spec, pl.BlockSpec(memory_space=pltpu.VMEM)),
+        in_specs=[pl.BlockSpec(memory_space=pltpu.SMEM)] + [hbm_spec] * 10,
+        out_specs=(hbm_spec, vmem_spec),
         scratch_shapes=[
             pltpu.VMEM((users, span, embed), BF16),
             pltpu.VMEM((users, span), jnp.int32),
@@ -496,7 +512,7 @@
             pltpu.VMEM((1, width), F32),
             pltpu.VMEM((4, width, cols), BF16),
             pltpu.VMEM((1, cols), F32),
-            pltpu.VMEM((1, hidden), BF16),
+            pltpu.VMEM((hidden // 128, 128), BF16),
             pltpu.VMEM((n_head, cols, hidden), BF16),
             pltpu.VMEM((rows, width), BF16),
             pltpu.VMEM((users * cand, width), BF16),
@@ -530,7 +546,7 @@
             dma((n_head,)),
         ],
         compiler_params=pltpu.CompilerParams(
-            collective_id=0, has_side_effects=True, vmem_limit_bytes=48 * 1024 * 1024
+            collective_id=0, has_side_effects=True, vmem_limit_bytes=60 * 1024 * 1024
         ),
         cost_estimate=pl.CostEstimate(
             flops=flops, bytes_accessed=6 * 1024 * 1024, transcendentals=0
@@ -546,7 +562,7 @@
         proj_weight,
         output_gain.reshape(1, cols),
         ranker_first,
-        ranker_second.reshape(1, hidden),
+        ranker_second.reshape(hidden // 128, 128),
     )
     return history_out, scores
 

time: 36.9 us -> 28.8 us (0.78)
  local copies, waits for them, and re-layouts: 11.1 us -> 3.07 us
    unnamed x22 -> x2, local copies, waits for them, and re-layouts: 10.4 us -> 3.07 us
    reshape x1 -> x0, local copies, waits for them, and re-layouts: 0.69 us -> none  [local(): ranker_second.reshape(1, hidden)]
where the time goes in v2:
time: 28.8 us; the launch traced here: 28.6 us
  Pallas kernels  24.9 us (86%)
  local copies, waits for them, and re-layouts  3.07 us (11%)
  between operations  0.64 us (2%)
    pallas_call x1, Pallas kernels, local(): pl.pallas_call(functools.partial(kernel, n_ctx, n_head, chunk), out_shape...  24.9 us
    unnamed x2, local copies, waits for them, and re-layouts  3.07 us

profile of v2, /device:TPU:0, one launch (start us, length us, event | category | flops | bytes accessed | tf_op | source)
XLA Modules:
  0.0 28.6 jit_solution(7127253404323821693)
XLA Ops:
  0.6 24.9 %shard_map.122 = (bf16[2,512,256]{2,1,0:T(8,128)(2,1)}, f32[2,32]{1,0:T(2,128)}) custom-call(s32[2]{0:T(128)} %hl.1, bf16[2,512,256]{2,1,0:T(8,128)(2,1)} %be_h.1, s32[2,512]{1,0:T(2,128)} %mk_h.1, f32[2,2,512]{2,1,0:T(2,128)} %ld_h.1, bf16[2,128,256]{2,1,0:T(8,128)(2,1)} %ce_h.1, bf16[256,1024]{1,0:T(8,128)(2,1)} %iw_h.1, f32[1,1024]{1,0:T(1,128)} %bitcast.3, ...), custom_call_target="tpu_custom_call" | custom-call | flops 2684354560 | bytes 6291456 | tf_op jit(solution)/shard_map/pallas_call | solution.py:498
  25.5 1.9 %copy.15 = bf16[2,512,256]{2,1,0:T(8,128)(2,1)} copy(bf16[2,512,256]{2,1,0:T(8,128)(2,1)} %get-tuple-element.4) | data formatting | bytes 1048576
  27.4 1.2 %copy.16 = f32[2,32]{1,0:T(2,128)} copy(f32[2,32]{1,0:T(2,128)} %get-tuple-element.5) | data formatting | bytes 512

commit v3 on v2

--- a/solution.py
+++ b/solution.py
@@ -137,29 +137,8 @@
             barrier, inc=1, device_id={"head": lax.rem(hm + k, n_head)}, device_id_type=MESH
         )
 
-    pl.semaphore_wait(barrier, n_ctx + n_head - 2)
-
-    def rank_copy(slot, target, sem):
-        return pltpu.make_async_remote_copy(
-            src_ref=rank.at[slot],
-            dst_ref=rank.at[slot],
-            send_sem=r_send.at[sem],
-            recv_sem=r_recv.at[slot],
-            device_id={"head": target},
-            device_id_type=MESH,
-        )
-
-    sibling = hm + 1 - 2 * core
-    loads["rf"].wait()
-    rank_copies = []
-    for k in range(CORES, n_head, CORES):
-        rank_copies.append(rank_copy(hm, lax.rem(hm + k, n_head), k))
-        rank_copies[-1].start()
-    rank_copies.append(rank_copy(hm, sibling, 0))
-    rank_copies[-1].start()
-
-    loads["ld"].wait()
-    loads["mk"].wait()
+    for name in ("ld", "mk", "be", "iw", "ig", "k", "v"):
+        loads[name].wait()
     dat[...] = jnp.zeros_like(dat)
     for u in range(users):
         for h in range(heads):
@@ -195,6 +174,153 @@
     col = jnp.transpose(dat[...])
     tall[me] = jnp.broadcast_to(end_total, (8, 128))
 
+    def right_copy(p):
+        return pltpu.make_async_remote_copy(
+            src_ref=p_out.at[p],
+            dst_ref=p_in.at[p],
+            send_sem=p_send.at[p],
+            recv_sem=p_recv.at[p],
+            device_id={"ctx": lax.rem(me + 1, n_ctx)},
+            device_id_type=MESH,
+        )
+
+    def left_copy(p):
+        return pltpu.make_async_remote_copy(
+            src_ref=x_out.at[p],
+            dst_ref=x_in.at[p],
+            send_sem=x_send.at[p],
+            recv_sem=x_recv.at[p],
+            device_id={"ctx": lax.rem(me + n_ctx - 1, n_ctx)},
+            device_id_type=MESH,
+        )
+
+    last = n_ctx - 1
+
+    weight = iw[...]
+    gain = ig[...]
+    tri = lax.broadcasted_iota(jnp.int32, (chunk, chunk), 0) >= lax.broadcasted_iota(
+        jnp.int32, (chunk, chunk), 1
+    )
+
+    def place(u, c):
+        b = u * chunks + c
+        return slice(b * chunk, (b + 1) * chunk), slice(c * chunk, (c + 1) * chunk)
+
+    def keys_values(u, c):
+        r, rc = place(u, c)
+        rows = normed(be[u, rc, :], weight, gain)
+        norm_s[r, :] = rows
+        key = (mm(rows, pw[1]) * DH ** (-0.5)).astype(BF16)
+        val = mm(rows, pw[2]).astype(BF16)
+        key_s[r, :] = key
+        val_s[r, :] = val
+        for h in range(heads):
+            p = u * heads + h
+            hc = slice(h * DH, (h + 1) * DH)
+            kw = (key[:, hc].astype(F32) * col[rc, 8 + p : 9 + p]).astype(BF16)
+            lst[p, c] = mm_tn(kw, val[:, hc])
+
+    def local_states(u):
+        for p in range(u * heads, (u + 1) * heads):
+            total = lst[p, 0]
+            for c in range(1, chunks):
+                total = total * fades[c][p : p + 1, :] + lst[p, c]
+            loc[p] = total
+
+    def first_sends(u):
+        @pl.when(me == 0)
+        def _():
+            for p in range(u * heads, (u + 1) * heads):
+                p_out[p] = loc[p].astype(p_out.dtype)
+                if n_ctx > 1:
+                    right_copy(p).start()
+
+        @pl.when(me == last)
+        def _():
+            for p in range(u * heads, (u + 1) * heads):
+                x_out[p] = loc[p].astype(x_out.dtype)
+                if n_ctx > 1:
+                    left_copy(p).start()
+
+    def relay_right(u):
+        for p in range(u * heads, (u + 1) * heads):
+            right_copy(p).wait_recv()
+
+            @pl.when(me < last)
+            def _():
+                p_out[p] = (
+                    p_in[p].astype(F32) * fade_total[p : p + 1, :] + loc[p]
+                ).astype(p_out.dtype)
+                right_copy(p).start()
+
+    def relay_left(u):
+        for p in range(u * heads, (u + 1) * heads):
+            left_copy(p).wait_recv()
+
+            @pl.when(me > 0)
+            def _():
+                x_out[p] = (
+                    x_in[p].astype(F32) + loc[p] * fade_after[p : p + 1, :]
+                ).astype(x_out.dtype)
+                left_copy(p).start()
+
+    half = n_ctx // 2
+
+    def near_relay(u):
+        if n_ctx > 1:
+
+            @pl.when((me > 0) & (me < half))
+            def _():
+                relay_right(u)
+
+            @pl.when((me < last) & (me >= half))
+            def _():
+                relay_left(u)
+
+    def far_relay(u, ends):
+        if n_ctx > 1:
+            at_end = (me == 0) | (me == last)
+            turn = at_end if ends else jnp.logical_not(at_end)
+
+            @pl.when(turn & (me < half))
+            def _():
+                relay_left(u)
+
+            @pl.when(turn & (me >= half))
+            def _():
+                relay_right(u)
+
+    def queries_gates(u):
+        for c in range(chunks):
+            r, _ = place(u, c)
+            rows = norm_s[r, :]
+            qry_s[r, :] = mm(rows, pw[0]).astype(BF16)
+            gate_s[r, :] = silu(mm(rows, pw[3]).astype(BF16).astype(F32)) * out_gain
+
+    def attention(u):
+        for c in range(chunks):
+            r, rc = place(u, c)
+            seen = tri & (valid[u][:, rc] > 0.5)
+            for h in range(heads):
+                p = u * heads + h
+                hc = slice(h * DH, (h + 1) * DH)
+                gap = col[rc, p : p + 1] - dat[p : p + 1, rc]
+                decay = jnp.where(seen, jnp.exp(jnp.where(tri, gap, 0.0)), 0.0)
+                att = (mm_nt(qry_s[r, hc], key_s[r, hc]) * decay).astype(BF16)
+                within_s[r, hc] = mm(att, val_s[r, hc])
+
+    keys_values(0, 0)
+
+    pl.semaphore_wait(barrier, n_ctx + n_head - 2)
+
+    @pl.when(me == 0)
+    def _():
+        p_in[...] = jnp.zeros_like(p_in)
+
+    @pl.when(me == last)
+    def _():
+        x_in[...] = jnp.zeros_like(x_in)
+
     t_copies = []
     for k in range(1, n_ctx):
         cp = pltpu.make_async_remote_copy(
@@ -208,90 +334,31 @@
         cp.start()
         t_copies.append(cp)
 
-    def right_copy(p):
+    def rank_copy(slot, target, sem):
         return pltpu.make_async_remote_copy(
-            src_ref=p_out.at[p],
-            dst_ref=p_in.at[p],
-            send_sem=p_send.at[p],
-            recv_sem=p_recv.at[p],
-            device_id={"ctx": lax.rem(me + 1, n_ctx)},
+            src_ref=rank.at[slot],
+            dst_ref=rank.at[slot],
+            send_sem=r_send.at[sem],
+            recv_sem=r_recv.at[slot],
+            device_id={"head": target},
             device_id_type=MESH,
         )
 
-    def left_copy(p):
-        return pltpu.make_async_remote_copy(
-            src_ref=x_out.at[p],
-            dst_ref=x_in.at[p],
-            send_sem=x_send.at[p],
-            recv_sem=x_recv.at[p],
-            device_id={"ctx": lax.rem(me + n_ctx - 1, n_ctx)},
-            device_id_type=MESH,
-        )
-
-    last = n_ctx - 1
-
-    @pl.when(me == 0)
-    def _():
-        p_in[...] = jnp.zeros_like(p_in)
-
-    @pl.when(me == last)
-    def _():
-        x_in[...] = jnp.zeros_like(x_in)
-
-    loads["be"].wait()
-    loads["iw"].wait()
-    loads["ig"].wait()
-    loads["k"].wait()
-    loads["v"].wait()
-    weight = iw[...]
-    gain = ig[...]
-    blocks = [(u, c) for u in range(users) for c in range(chunks)]
+    sibling = hm + 1 - 2 * core
+    loads["rf"].wait()
+    rank_copies = []
+    for k in range(CORES, n_head, CORES):
+        rank_copies.append(rank_copy(hm, lax.rem(hm + k, n_head), k))
+        rank_copies[-1].start()
+    rank_copies.append(rank_copy(hm, sibling, 0))
+    rank_copies[-1].start()
+
     for u in range(users):
         for c in range(chunks):
-            b = u * chunks + c
-            r = slice(b * chunk, (b + 1) * chunk)
-            rc = slice(c * chunk, (c + 1) * chunk)
-            rows = normed(be[u, rc, :], weight, gain)
-            norm_s[r, :] = rows
-            key = (mm(rows, pw[1]) * DH ** (-0.5)).astype(BF16)
-            val = mm(rows, pw[2]).astype(BF16)
-            key_s[r, :] = key
-            val_s[r, :] = val
-            for h in range(heads):
-                p = u * heads + h
-                hc = slice(h * DH, (h + 1) * DH)
-                kw = (key[:, hc].astype(F32) * col[rc, 8 + p : 9 + p]).astype(BF16)
-                lst[p, c] = mm_tn(kw, val[:, hc])
-        mine = range(u * heads, (u + 1) * heads)
-        for p in mine:
-            total = lst[p, 0]
-            for c in range(1, chunks):
-                total = total * fades[c][p : p + 1, :] + lst[p, c]
-            loc[p] = total
-
-        @pl.when(me == 0)
-        def _():
-            for p in mine:
-                p_out[p] = loc[p].astype(p_out.dtype)
-                if n_ctx > 1:
-                    right_copy(p).start()
-
-        @pl.when(me == last)
-        def _():
-            for p in mine:
-                x_out[p] = loc[p].astype(x_out.dtype)
-                if n_ctx > 1:
-                    left_copy(p).start()
-
-    loads["q"].wait()
-    loads["g"].wait()
-    loads["og"].wait()
-    out_gain = og[...]
-    for b in range(len(blocks)):
-        r = slice(b * chunk, (b + 1) * chunk)
-        rows = norm_s[r, :]
-        qry_s[r, :] = mm(rows, pw[0]).astype(BF16)
-        gate_s[r, :] = silu(mm(rows, pw[3]).astype(BF16).astype(F32)) * out_gain
+            if u + c > 0:
+                keys_values(u, c)
+        local_states(u)
+        first_sends(u)
 
     for k in range(1, n_ctx):
         src = lax.rem(me + n_ctx - k, n_ctx)
@@ -308,69 +375,24 @@
         after = after + jnp.where(j > me, tall[j], 0.0)
     fade_after = jnp.exp(after)[:, 0:1]
 
-    def relay_right():
-        for p in range(pairs):
-            right_copy(p).wait_recv()
-
-            @pl.when(me < last)
-            def _():
-                p_out[p] = (
-                    p_in[p].astype(F32) * fade_total[p : p + 1, :] + loc[p]
-                ).astype(p_out.dtype)
-                right_copy(p).start()
-
-    def relay_left():
-        for p in range(pairs):
-            left_copy(p).wait_recv()
-
-            @pl.when(me > 0)
-            def _():
-                x_out[p] = (
-                    x_in[p].astype(F32) + loc[p] * fade_after[p : p + 1, :]
-                ).astype(x_out.dtype)
-                left_copy(p).start()
-
-    half = n_ctx // 2
-    if n_ctx > 1:
-
-        @pl.when((me > 0) & (me < half))
-        def _():
-            relay_right()
-
-        @pl.when((me < last) & (me >= half))
-        def _():
-            relay_left()
-
-    tri = lax.broadcasted_iota(jnp.int32, (chunk, chunk), 0) >= lax.broadcasted_iota(
-        jnp.int32, (chunk, chunk), 1
-    )
-    for b, (u, c) in enumerate(blocks):
-        r = slice(b * chunk, (b + 1) * chunk)
-        rc = slice(c * chunk, (c + 1) * chunk)
-        seen = tri & (valid[u][:, rc] > 0.5)
-        for h in range(heads):
-            p = u * heads + h
-            hc = slice(h * DH, (h + 1) * DH)
-            gap = col[rc, p : p + 1] - dat[p : p + 1, rc]
-            decay = jnp.where(seen, jnp.exp(jnp.where(tri, gap, 0.0)), 0.0)
-            att = (mm_nt(qry_s[r, hc], key_s[r, hc]) * decay).astype(BF16)
-            within_s[r, hc] = mm(att, val_s[r, hc])
-
-    loads["ce"].wait()
-    loads["r2"].wait()
+    for name in ("q", "g", "og", "ce", "r2"):
+        loads[name].wait()
+    out_gain = og[...]
+    near_relay(0)
+    for u in range(users):
+        queries_gates(u)
+        if u + 1 < users:
+            near_relay(u + 1)
+    far_relay(0, False)
+    for u in range(users):
+        attention(u)
+        if u + 1 < users:
+            far_relay(u + 1, False)
     cnorm[...] = normed(ce[...].reshape(users * cand, ce.shape[2]), weight, gain)
     cand_q = mm(cnorm[...], pw[0]).astype(BF16)
     own = cnorm[:, pl.ds(pl.multiple_of(hm * cols, DH), cols)].astype(F32)
-
-    if n_ctx > 1:
-
-        @pl.when((me < last) & (me < half))
-        def _():
-            relay_left()
-
-        @pl.when((me > 0) & (me >= half))
-        def _():
-            relay_right()
+    for u in range(users):
+        far_relay(u, True)
 
     for p in range(pairs):
         u, h = p // heads, p % heads
@@ -462,6 +484,19 @@
                 left_copy(p).wait_send()
 
     for cp in out_copies:
+        cp.wait()
+
+
+def results(hist_i, score_i, hist_o, score_o, sem):
+    copies = [
+        pltpu.make_async_copy(score_i, score_o, sem.at[0]),
+    ]
+    users = hist_i.shape[0]
+    for u in range(users):
+        copies.append(pltpu.make_async_copy(hist_i.at[u], hist_o.at[u], sem.at[u + 1]))
+    for cp in copies:
+        cp.start()
+    for cp in copies:
         cp.wait()
 
 
@@ -564,7 +599,18 @@
         ranker_first,
         ranker_second.reshape(hidden // 128, 128),
     )
-    return history_out, scores
+    return pl.pallas_call(
+        results,
+        out_shape=(
+            jax.ShapeDtypeStruct(history_out.shape, BF16),
+            jax.ShapeDtypeStruct(scores.shape, F32),
+        ),
+        in_specs=[hbm_spec, hbm_spec],
+        out_specs=(hbm_spec, hbm_spec),
+        scratch_shapes=[dma((users + 1,))],
+        compiler_params=pltpu.CompilerParams(vmem_limit_bytes=60 * 1024 * 1024),
+        cost_estimate=pl.CostEstimate(flops=0, bytes_accessed=1024 * 1024, transcendentals=0),
+    )(history_out, scores)
 
 
 def solution(mesh):

time: 28.8 us -> 42.4 us (1.47)
  Pallas kernels: 24.9 us -> 41.6 us
  local copies, waits for them, and re-layouts: 3.07 us -> 0 us
    pallas_call x0 -> x1, Pallas kernels: none -> 17 us  [local(): pl.pallas_call(results, out_shape=(jax.ShapeDtypeStruct(history_out.shape...]
    unnamed x2 -> x0, local copies, waits for them, and re-layouts: 3.07 us -> none
where the time goes in v3:
time: 42.4 us; the launch traced here: 42.3 us
  Pallas kernels  41.6 us (98%)
  between operations  0.64 us (2%)
    pallas_call x1, Pallas kernels, local(): pl.pallas_call(functools.partial(kernel, n_ctx, n_head, chunk), out_shape...  24.6 us
    pallas_call x1, Pallas kernels, local(): pl.pallas_call(results, out_shape=(jax.ShapeDtypeStruct(history_out.shape...  17 us

profile of v3, /device:TPU:0, one launch (start us, length us, event | category | flops | bytes accessed | tf_op | source)
XLA Modules:
  0.0 42.3 jit_solution(12433165116381576763)
XLA Ops:
  0.6 24.6 %shard_map.122 = (bf16[2,512,256]{2,1,0:T(8,128)(2,1)}, f32[2,32]{1,0:T(2,128)}) custom-call(s32[2]{0:T(128)} %hl.1, bf16[2,512,256]{2,1,0:T(8,128)(2,1)} %be_h.1, s32[2,512]{1,0:T(2,128)} %mk_h.1, f32[2,2,512]{2,1,0:T(2,128)} %ld_h.1, bf16[2,128,256]{2,1,0:T(8,128)(2,1)} %ce_h.1, bf16[256,1024]{1,0:T(8,128)(2,1)} %iw_h.1, f32[1,1024]{1,0:T(1,128)} %bitcast.3, ...), custom_call_target="tpu_custom_call" | custom-call | flops 2684354560 | bytes 6291456 | tf_op jit(solution)/shard_map/pallas_call | solution.py:533
  25.2 17.0 %shard_map.123 = (bf16[2,512,256]{2,1,0:T(8,128)(2,1)}, f32[2,32]{1,0:T(2,128)}) custom-call(bf16[2,512,256]{2,1,0:T(8,128)(2,1)} %get-tuple-element.4.hist_i, f32[2,32]{1,0:T(2,128)} %get-tuple-element.5.score_i), custom_call_target="tpu_custom_call" | custom-call | bytes 1048576 | tf_op jit(solution)/shard_map/pallas_call | solution.py:602

commit v4 on v3

--- a/solution.py
+++ b/solution.py
@@ -52,7 +52,7 @@
     og_h,
     rf_h,
     r2_h,
-    hist_h,
+    hist,
     score_o,
     be,
     mk,
@@ -71,7 +71,6 @@
     qry_s,
     gate_s,
     within_s,
-    hist,
     dat,
     lst,
     loc,
@@ -83,7 +82,6 @@
     feat,
     feat_in,
     load_sem,
-    out_sem,
     t_send,
     t_recv,
     p_send,
@@ -109,7 +107,6 @@
     loads = {}
     for i, (name, src, dst) in enumerate(
         (
-            ("rf", rf_h, rank.at[hm]),
             ("be", be_h, be),
             ("iw", iw_h, iw),
             ("ig", ig_h, ig),
@@ -122,6 +119,7 @@
             ("og", og_h, og),
             ("ce", ce_h, ce),
             ("r2", r2_h, r2),
+            ("rf", rf_h, rank.at[hm]),
         )
     ):
         loads[name] = pltpu.make_async_copy(src, dst, load_sem.at[i])
@@ -136,6 +134,26 @@
         pl.semaphore_signal(
             barrier, inc=1, device_id={"head": lax.rem(hm + k, n_head)}, device_id_type=MESH
         )
+
+    pl.semaphore_wait(barrier, n_ctx + n_head - 2)
+
+    def rank_copy(slot, target, sem, src=None):
+        return pltpu.make_async_remote_copy(
+            src_ref=rank.at[slot] if src is None else src,
+            dst_ref=rank.at[slot],
+            send_sem=r_send.at[sem],
+            recv_sem=r_recv.at[slot],
+            device_id={"head": target},
+            device_id_type=MESH,
+        )
+
+    sibling = hm + 1 - 2 * core
+    rank_copies = []
+    for k in range(CORES, n_head, CORES):
+        rank_copies.append(rank_copy(hm, lax.rem(hm + k, n_head), k, rf_h))
+        rank_copies[-1].start()
+    rank_copies.append(rank_copy(hm, sibling, 0, rf_h))
+    rank_copies[-1].start()
 
     for name in ("ld", "mk", "be", "iw", "ig", "k", "v"):
         loads[name].wait()
@@ -309,10 +327,6 @@
                 att = (mm_nt(qry_s[r, hc], key_s[r, hc]) * decay).astype(BF16)
                 within_s[r, hc] = mm(att, val_s[r, hc])
 
-    keys_values(0, 0)
-
-    pl.semaphore_wait(barrier, n_ctx + n_head - 2)
-
     @pl.when(me == 0)
     def _():
         p_in[...] = jnp.zeros_like(p_in)
@@ -334,29 +348,9 @@
         cp.start()
         t_copies.append(cp)
 
-    def rank_copy(slot, target, sem):
-        return pltpu.make_async_remote_copy(
-            src_ref=rank.at[slot],
-            dst_ref=rank.at[slot],
-            send_sem=r_send.at[sem],
-            recv_sem=r_recv.at[slot],
-            device_id={"head": target},
-            device_id_type=MESH,
-        )
-
-    sibling = hm + 1 - 2 * core
-    loads["rf"].wait()
-    rank_copies = []
-    for k in range(CORES, n_head, CORES):
-        rank_copies.append(rank_copy(hm, lax.rem(hm + k, n_head), k))
-        rank_copies[-1].start()
-    rank_copies.append(rank_copy(hm, sibling, 0))
-    rank_copies[-1].start()
-
     for u in range(users):
         for c in range(chunks):
-            if u + c > 0:
-                keys_values(u, c)
+            keys_values(u, c)
         local_states(u)
         first_sends(u)
 
@@ -375,7 +369,7 @@
         after = after + jnp.where(j > me, tall[j], 0.0)
     fade_after = jnp.exp(after)[:, 0:1]
 
-    for name in ("q", "g", "og", "ce", "r2"):
+    for name in ("q", "g", "og", "ce", "r2", "rf"):
         loads[name].wait()
     out_gain = og[...]
     near_relay(0)
@@ -424,7 +418,6 @@
         rank_copies.append(rank_copy(src, sibling, n_head + k))
         rank_copies[-1].start()
 
-    out_copies = []
     for u in range(users):
         for h in range(heads):
             p = u * heads + h
@@ -440,8 +433,6 @@
                 hist[u, rc, hc] = (read * scale * gate_s[r, hc]).astype(BF16)
                 if c + 1 < chunks:
                     state = state * fades[c][p : p + 1, :] + lst[p, c]
-        out_copies.append(pltpu.make_async_copy(hist.at[u], hist_h.at[u], out_sem.at[u]))
-        out_copies[-1].start()
 
     mine = feat[:, pl.ds(pl.multiple_of(hm * share, share), share), :]
     hidden = mm(mine.reshape(users * share, cols), rank[hm])
@@ -482,9 +473,6 @@
         def _():
             for p in range(pairs):
                 left_copy(p).wait_send()
-
-    for cp in out_copies:
-        cp.wait()
 
 
 def results(hist_i, score_i, hist_o, score_o, sem):
@@ -533,11 +521,11 @@
     history_out, scores = pl.pallas_call(
         functools.partial(kernel, n_ctx, n_head, chunk),
         out_shape=(
-            jax.ShapeDtypeStruct((users, span, cols), BF16),
-            jax.ShapeDtypeStruct((users, share), F32),
+            pltpu.VMEM((users, span, cols), BF16),
+            pltpu.VMEM((users, share), F32),
         ),
         in_specs=[pl.BlockSpec(memory_space=pltpu.SMEM)] + [hbm_spec] * 10,
-        out_specs=(hbm_spec, vmem_spec),
+        out_specs=(vmem_spec, vmem_spec),
         scratch_shapes=[
             pltpu.VMEM((users, span, embed), BF16),
             pltpu.VMEM((users, span), jnp.int32),
@@ -556,7 +544,6 @@
             pltpu.VMEM((rows, cols), BF16),
             pltpu.VMEM((rows, cols), F32),
             pltpu.VMEM((rows, cols), F32),
-            pltpu.VMEM((users, span, cols), BF16),
             pltpu.VMEM((24, span), F32),
             pltpu.VMEM((pairs, chunks, DH, DH), F32),
             pltpu.VMEM((pairs, DH, DH), F32),
@@ -568,7 +555,6 @@
             pltpu.VMEM((users, cand, cols), BF16),
             pltpu.VMEM((n_head, users, share, cols), BF16),
             dma((13,)),
-            dma((users,)),
             dma((n_ctx,)),
             dma((n_ctx,)),
             dma((pairs,)),
@@ -605,10 +591,10 @@
             jax.ShapeDtypeStruct(history_out.shape, BF16),
             jax.ShapeDtypeStruct(scores.shape, F32),
         ),
-        in_specs=[hbm_spec, hbm_spec],
+        in_specs=[vmem_spec, vmem_spec],
         out_specs=(hbm_spec, hbm_spec),
         scratch_shapes=[dma((users + 1,))],
-        compiler_params=pltpu.CompilerParams(vmem_limit_bytes=60 * 1024 * 1024),
+        compiler_params=pltpu.CompilerParams(vmem_limit_bytes=8 * 1024 * 1024),
         cost_estimate=pl.CostEstimate(flops=0, bytes_accessed=1024 * 1024, transcendentals=0),
     )(history_out, scores)
 

time: 42.4 us -> 25.6 us (0.60)
  Pallas kernels: 41.6 us -> 24.8 us
    pallas_call x1, Pallas kernels: 17 us -> 0.82 us  [local(): pl.pallas_call(results, out_shape=(jax.ShapeDtypeStruct(history_out.shape...]
    pallas_call x1, Pallas kernels: 24.6 us -> 24 us  [local(): pl.pallas_call(functools.partial(kernel, n_ctx, n_head, chunk), out_shape...]
where the time goes in v4:
time: 25.6 us; the launch traced here: 25.5 us
  Pallas kernels  24.8 us (97%)
  between operations  0.64 us (2%)
    pallas_call x1, Pallas kernels, local(): pl.pallas_call(functools.partial(kernel, n_ctx, n_head, chunk), out_shape...  24 us
    pallas_call x1, Pallas kernels, local(): pl.pallas_call(results, out_shape=(jax.ShapeDtypeStruct(history_out.shape...  0.82 us

profile of v4, /device:TPU:0, one launch (start us, length us, event | category | flops | bytes accessed | tf_op | source)
XLA Modules:
  0.0 25.5 jit_solution(16782539246433158764)
XLA Ops:
  0.6 24.0 %shard_map.122 = (bf16[2,512,256]{2,1,0:T(8,128)(2,1)S(1)}, f32[2,32]{1,0:T(2,128)S(1)}) custom-call(s32[2]{0:T(128)} %hl.1, bf16[2,512,256]{2,1,0:T(8,128)(2,1)} %be_h.1, s32[2,512]{1,0:T(2,128)} %mk_h.1, f32[2,2,512]{2,1,0:T(2,128)} %ld_h.1, bf16[2,128,256]{2,1,0:T(8,128)(2,1)} %ce_h.1, bf16[256,1024]{1,0:T(8,128)(2,1)} %iw_h.1, f32[1,1024]{1,0:T(1,128)} %bitcast.3, ...), custom_call_target="tpu_custom_call" | custom-call | flops 2684354560 | bytes 6291456 | tf_op jit(solution)/shard_map/pallas_call | solution.py:521
  24.6 0.8 %shard_map.123 = (bf16[2,512,256]{2,1,0:T(8,128)(2,1)}, f32[2,32]{1,0:T(2,128)}) custom-call(bf16[2,512,256]{2,1,0:T(8,128)(2,1)S(1)} %get-tuple-element.4.hist_i, f32[2,32]{1,0:T(2,128)S(1)} %get-tuple-element.5.score_i), custom_call_target="tpu_custom_call" | custom-call | bytes 1048576 | tf_op jit(solution)/shard_map/pallas_call | solution.py:588

commit v5 on v4

--- a/solution.py
+++ b/solution.py
@@ -224,19 +224,19 @@
         b = u * chunks + c
         return slice(b * chunk, (b + 1) * chunk), slice(c * chunk, (c + 1) * chunk)
 
-    def keys_values(u, c):
-        r, rc = place(u, c)
-        rows = normed(be[u, rc, :], weight, gain)
-        norm_s[r, :] = rows
-        key = (mm(rows, pw[1]) * DH ** (-0.5)).astype(BF16)
-        val = mm(rows, pw[2]).astype(BF16)
-        key_s[r, :] = key
-        val_s[r, :] = val
+    def keys_values(u):
+        ru = slice(u * span, (u + 1) * span)
+        rows = normed(be[u], weight, gain)
+        norm_s[ru, :] = rows
+        key_s[ru, :] = (mm(rows, pw[1]) * DH ** (-0.5)).astype(BF16)
+        val_s[ru, :] = mm(rows, pw[2]).astype(BF16)
         for h in range(heads):
             p = u * heads + h
             hc = slice(h * DH, (h + 1) * DH)
-            kw = (key[:, hc].astype(F32) * col[rc, 8 + p : 9 + p]).astype(BF16)
-            lst[p, c] = mm_tn(kw, val[:, hc])
+            for c in range(chunks):
+                r, rc = place(u, c)
+                kw = (key_s[r, hc].astype(F32) * col[rc, 8 + p : 9 + p]).astype(BF16)
+                lst[p, c] = mm_tn(kw, val_s[r, hc])
 
     def local_states(u):
         for p in range(u * heads, (u + 1) * heads):
@@ -309,11 +309,10 @@
                 relay_right(u)
 
     def queries_gates(u):
-        for c in range(chunks):
-            r, _ = place(u, c)
-            rows = norm_s[r, :]
-            qry_s[r, :] = mm(rows, pw[0]).astype(BF16)
-            gate_s[r, :] = silu(mm(rows, pw[3]).astype(BF16).astype(F32)) * out_gain
+        ru = slice(u * span, (u + 1) * span)
+        rows = norm_s[ru, :]
+        qry_s[ru, :] = mm(rows, pw[0]).astype(BF16)
+        gate_s[ru, :] = silu(mm(rows, pw[3]).astype(BF16).astype(F32)) * out_gain
 
     def attention(u):
         for c in range(chunks):
@@ -349,8 +348,7 @@
         t_copies.append(cp)
 
     for u in range(users):
-        for c in range(chunks):
-            keys_values(u, c)
+        keys_values(u)
         local_states(u)
         first_sends(u)
 
@@ -375,57 +373,47 @@
     near_relay(0)
     for u in range(users):
         queries_gates(u)
-        if u + 1 < users:
-            near_relay(u + 1)
+    for u in range(1, users):
+        near_relay(u)
     far_relay(0, False)
-    for u in range(users):
-        attention(u)
-        if u + 1 < users:
-            far_relay(u + 1, False)
+    attention(0)
     cnorm[...] = normed(ce[...].reshape(users * cand, ce.shape[2]), weight, gain)
     cand_q = mm(cnorm[...], pw[0]).astype(BF16)
     own = cnorm[:, pl.ds(pl.multiple_of(hm * cols, DH), cols)].astype(F32)
-    for u in range(users):
-        far_relay(u, True)
-
-    for p in range(pairs):
-        u, h = p // heads, p % heads
-        hc = slice(h * DH, (h + 1) * DH)
+    for u in range(1, users):
+        far_relay(u, False)
+
+    def candidates(u):
         rows = slice(u * cand, (u + 1) * cand)
-        state = p_in[p].astype(F32) * fade_total[p : p + 1, :] + loc[p]
-        state = state * fade_after[p : p + 1, :] + x_in[p].astype(F32)
-        read = mm(cand_q[rows, hc], state.astype(BF16))
-        scale = lax.rsqrt(jnp.mean(read * read, axis=-1, keepdims=True) + EPS)
-        feat[u, :, hc] = (read * scale * out_gain[:, hc] + own[rows, hc]).astype(BF16)
-
-    def feat_copy(k):
+        for h in range(heads):
+            p = u * heads + h
+            hc = slice(h * DH, (h + 1) * DH)
+            state = p_in[p].astype(F32) * fade_total[p : p + 1, :] + loc[p]
+            state = state * fade_after[p : p + 1, :] + x_in[p].astype(F32)
+            read = mm(cand_q[rows, hc], state.astype(BF16))
+            scale = lax.rsqrt(jnp.mean(read * read, axis=-1, keepdims=True) + EPS)
+            feat[u, :, hc] = (read * scale * out_gain[:, hc] + own[rows, hc]).astype(BF16)
+        for k in range(1, n_head):
+            feat_copy(u, k).start()
+
+    def feat_copy(u, k):
         target = lax.rem(hm + k, n_head)
         return pltpu.make_async_remote_copy(
-            src_ref=feat.at[:, pl.ds(pl.multiple_of(target * share, share), share), :],
-            dst_ref=feat_in.at[hm],
-            send_sem=f_send.at[k],
-            recv_sem=f_recv.at[hm],
+            src_ref=feat.at[u, pl.ds(pl.multiple_of(target * share, share), share), :],
+            dst_ref=feat_in.at[hm, u],
+            send_sem=f_send.at[u, k],
+            recv_sem=f_recv.at[u, hm],
             device_id={"head": target},
             device_id_type=MESH,
         )
 
-    for k in range(1, n_head):
-        feat_copy(k).start()
-
-    for k in range(CORES, n_head, CORES):
-        src = lax.rem(hm + n_head - k, n_head)
-        rank_copy(src, sibling, k).wait_recv()
-        rank_copies.append(rank_copy(src, sibling, n_head + k))
-        rank_copies[-1].start()
-
-    for u in range(users):
+    def histories(u):
         for h in range(heads):
             p = u * heads + h
             hc = slice(h * DH, (h + 1) * DH)
             state = p_in[p].astype(F32)
             for c in range(chunks):
-                r = slice((u * chunks + c) * chunk, (u * chunks + c + 1) * chunk)
-                rc = slice(c * chunk, (c + 1) * chunk)
+                r, rc = place(u, c)
                 read = within_s[r, hc] + col[rc, 16 + p : 17 + p] * mm(
                     qry_s[r, hc], state.astype(BF16)
                 )
@@ -433,6 +421,21 @@
                 hist[u, rc, hc] = (read * scale * gate_s[r, hc]).astype(BF16)
                 if c + 1 < chunks:
                     state = state * fades[c][p : p + 1, :] + lst[p, c]
+
+    for u in range(users):
+        far_relay(u, True)
+        candidates(u)
+        if u + 1 < users:
+            attention(u + 1)
+            histories(u)
+
+    for k in range(CORES, n_head, CORES):
+        src = lax.rem(hm + n_head - k, n_head)
+        rank_copy(src, sibling, k).wait_recv()
+        rank_copies.append(rank_copy(src, sibling, n_head + k))
+        rank_copies[-1].start()
+
+    histories(users - 1)
 
     mine = feat[:, pl.ds(pl.multiple_of(hm * share, share), share), :]
     hidden = mm(mine.reshape(users * share, cols), rank[hm])
@@ -442,14 +445,15 @@
         rank_copy(src, sibling, n_head + k).wait_recv()
     for k in range(1, n_head):
         src = lax.rem(hm + n_head - k, n_head)
-        pltpu.make_async_remote_copy(
-            src_ref=feat_in.at[src],
-            dst_ref=feat_in.at[src],
-            send_sem=f_send.at[k],
-            recv_sem=f_recv.at[src],
-            device_id={"head": src},
-            device_id_type=MESH,
-        ).wait_recv()
+        for u in range(users):
+            pltpu.make_async_remote_copy(
+                src_ref=feat_in.at[src, u],
+                dst_ref=feat_in.at[src, u],
+                send_sem=f_send.at[u, k],
+                recv_sem=f_recv.at[u, src],
+                device_id={"head": src},
+                device_id_type=MESH,
+            ).wait_recv()
         hidden = hidden + mm(feat_in[src].reshape(users * share, cols), rank[src])
     second = r2[...].astype(F32)
     acted = silu(hidden)
@@ -460,8 +464,9 @@
 
     for cp in t_copies + rank_copies:
         cp.wait_send()
-    for k in range(1, n_head):
-        feat_copy(k).wait_send()
+    for u in range(users):
+        for k in range(1, n_head):
+            feat_copy(u, k).wait_send()
     if n_ctx > 1:
 
         @pl.when(me < last)
@@ -563,8 +568,8 @@
             dma((pairs,)),
             dma((2 * n_head,)),
             dma((n_head,)),
-            dma((n_head,)),
-            dma((n_head,)),
+            dma((users, n_head)),
+            dma((users, n_head)),
         ],
         compiler_params=pltpu.CompilerParams(
             collective_id=0, has_side_effects=True, vmem_limit_bytes=60 * 1024 * 1024

time: 25.6 us -> 25.2 us (0.984)
  Pallas kernels: 24.8 us -> 24.4 us
    pallas_call x1, Pallas kernels: 24 us -> 23.6 us  [local(): pl.pallas_call(functools.partial(kernel, n_ctx, n_head, chunk), out_shape...]
where the time goes in v5:
time: 25.2 us; the launch traced here: 25 us
  Pallas kernels  24.4 us (97%)
  between operations  0.64 us (3%)
    pallas_call x1, Pallas kernels, local(): pl.pallas_call(functools.partial(kernel, n_ctx, n_head, chunk), out_shape...  23.6 us
    pallas_call x1, Pallas kernels, local(): pl.pallas_call(results, out_shape=(jax.ShapeDtypeStruct(history_out.shape...  0.82 us

profile of v5, /device:TPU:0, one launch (start us, length us, event | category | flops | bytes accessed | tf_op | source)
XLA Modules:
  0.0 25.0 jit_solution(9047955425559993476)
XLA Ops:
  0.6 23.6 %shard_map.122 = (bf16[2,512,256]{2,1,0:T(8,128)(2,1)S(1)}, f32[2,32]{1,0:T(2,128)S(1)}) custom-call(s32[2]{0:T(128)} %hl.1, bf16[2,512,256]{2,1,0:T(8,128)(2,1)} %be_h.1, s32[2,512]{1,0:T(2,128)} %mk_h.1, f32[2,2,512]{2,1,0:T(2,128)} %ld_h.1, bf16[2,128,256]{2,1,0:T(8,128)(2,1)} %ce_h.1, bf16[256,1024]{1,0:T(8,128)(2,1)} %iw_h.1, f32[1,1024]{1,0:T(1,128)} %bitcast.3, ...), custom_call_target="tpu_custom_call" | custom-call | flops 2684354560 | bytes 6291456 | tf_op jit(solution)/shard_map/pallas_call | solution.py:526
  24.2 0.8 %shard_map.123 = (bf16[2,512,256]{2,1,0:T(8,128)(2,1)}, f32[2,32]{1,0:T(2,128)}) custom-call(bf16[2,512,256]{2,1,0:T(8,128)(2,1)S(1)} %get-tuple-element.4.hist_i, f32[2,32]{1,0:T(2,128)S(1)} %get-tuple-element.5.score_i), custom_call_target="tpu_custom_call" | custom-call | bytes 1048576 | tf_op jit(solution)/shard_map/pallas_call | solution.py:593

commit v6 on v5

--- a/solution.py
+++ b/solution.py
@@ -38,6 +38,7 @@
 
 
 def kernel(
+    n_grp,
     n_ctx,
     n_head,
     chunk,
@@ -90,6 +91,12 @@
     x_recv,
     r_send,
     r_recv,
+    wx_send,
+    wx_recv,
+    wy_send,
+    wy_recv,
+    wf_send,
+    wf_recv,
     f_send,
     f_recv,
 ):
@@ -135,7 +142,12 @@
             barrier, inc=1, device_id={"head": lax.rem(hm + k, n_head)}, device_id_type=MESH
         )
 
-    pl.semaphore_wait(barrier, n_ctx + n_head - 2)
+    paired = n_grp == 2
+    if paired:
+        pl.semaphore_signal(
+            barrier, inc=1, device_id={"grp": 1 - lax.axis_index("grp")}, device_id_type=MESH
+        )
+    pl.semaphore_wait(barrier, n_ctx + n_head - 2 + int(paired))
 
     def rank_copy(slot, target, sem, src=None):
         return pltpu.make_async_remote_copy(
@@ -149,9 +161,56 @@
 
     sibling = hm + 1 - 2 * core
     rank_copies = []
-    for k in range(CORES, n_head, CORES):
-        rank_copies.append(rank_copy(hm, lax.rem(hm + k, n_head), k, rf_h))
-        rank_copies[-1].start()
+    mine_g = lax.axis_index("grp") if paired else 0
+    other_g = 1 - mine_g
+    nx, ny = (5, 3) if paired else (8, 0)
+    depth = cols // 8
+
+    def piece(slot, s, grp, target, send, recv, src=None):
+        rows = pl.ds(pl.multiple_of((s + grp * (7 - 2 * s)) * depth, depth), depth)
+        return pltpu.make_async_remote_copy(
+            src_ref=rank.at[slot, rows, :] if src is None else src.at[rows, :],
+            dst_ref=rank.at[slot, rows, :],
+            send_sem=send,
+            recv_sem=recv,
+            device_id=target,
+            device_id_type=MESH,
+        )
+
+    def along_x(slot, target, k, s, src=None):
+        return piece(
+            slot, s, mine_g, {"head": target}, wx_send.at[k, s], wx_recv.at[slot, s], src
+        )
+
+    def along_y(slot, k, s, grp):
+        return piece(slot, s, grp, {"grp": other_g}, wy_send.at[k, s], wy_recv.at[slot, s])
+
+    def to_sibling(slot, k, s, grp, i):
+        return piece(slot, s, grp, {"head": sibling}, wf_send.at[k, i], wf_recv.at[slot, i])
+
+    def pass_on(steps):
+        for s in steps:
+            for k in range(CORES, n_head, CORES):
+                slot = lax.rem(hm + n_head - k, n_head)
+                along_x(slot, slot, k, s).wait_recv()
+                if s < ny:
+                    rank_copies.append(along_y(slot, k, s, mine_g))
+                    rank_copies[-1].start()
+                rank_copies.append(to_sibling(slot, k, s, mine_g, s))
+                rank_copies[-1].start()
+
+    def pass_on_y(steps):
+        for s in steps:
+            for k in range(CORES, n_head, CORES):
+                slot = lax.rem(hm + n_head - k, n_head)
+                along_y(slot, k, s, other_g).wait_recv()
+                rank_copies.append(to_sibling(slot, k, s, other_g, nx + s))
+                rank_copies[-1].start()
+
+    for s in range(nx):
+        for k in range(CORES, n_head, CORES):
+            rank_copies.append(along_x(hm, lax.rem(hm + k, n_head), k, s, rf_h))
+            rank_copies[-1].start()
     rank_copies.append(rank_copy(hm, sibling, 0, rf_h))
     rank_copies[-1].start()
 
@@ -371,17 +430,21 @@
         loads[name].wait()
     out_gain = og[...]
     near_relay(0)
+    pass_on(range(0, 1))
     for u in range(users):
         queries_gates(u)
     for u in range(1, users):
         near_relay(u)
+    pass_on(range(1, 2))
     far_relay(0, False)
     attention(0)
+    pass_on(range(2, 3))
     cnorm[...] = normed(ce[...].reshape(users * cand, ce.shape[2]), weight, gain)
     cand_q = mm(cnorm[...], pw[0]).astype(BF16)
     own = cnorm[:, pl.ds(pl.multiple_of(hm * cols, DH), cols)].astype(F32)
     for u in range(1, users):
         far_relay(u, False)
+    pass_on(range(3, nx))
 
     def candidates(u):
         rows = slice(u * cand, (u + 1) * cand)
@@ -429,12 +492,7 @@
             attention(u + 1)
             histories(u)
 
-    for k in range(CORES, n_head, CORES):
-        src = lax.rem(hm + n_head - k, n_head)
-        rank_copy(src, sibling, k).wait_recv()
-        rank_copies.append(rank_copy(src, sibling, n_head + k))
-        rank_copies[-1].start()
-
+    pass_on_y(range(ny))
     histories(users - 1)
 
     mine = feat[:, pl.ds(pl.multiple_of(hm * share, share), share), :]
@@ -442,7 +500,10 @@
     rank_copy(sibling, sibling, 0).wait_recv()
     for k in range(CORES, n_head, CORES):
         src = lax.rem(sibling + n_head - k, n_head)
-        rank_copy(src, sibling, n_head + k).wait_recv()
+        for t in range(nx):
+            to_sibling(src, k, t, mine_g, t).wait_recv()
+        for t in range(ny):
+            to_sibling(src, k, t, other_g, nx + t).wait_recv()
     for k in range(1, n_head):
         src = lax.rem(hm + n_head - k, n_head)
         for u in range(users):
@@ -494,6 +555,7 @@
 
 
 def local(
+    n_grp,
     n_ctx,
     n_head,
     behavior_embed,
@@ -524,7 +586,7 @@
     vmem_spec = pl.BlockSpec(memory_space=pltpu.VMEM)
     flops = 2 * rows * width * (embed + 4 * cols)
     history_out, scores = pl.pallas_call(
-        functools.partial(kernel, n_ctx, n_head, chunk),
+        functools.partial(kernel, n_grp, n_ctx, n_head, chunk),
         out_shape=(
             pltpu.VMEM((users, span, cols), BF16),
             pltpu.VMEM((users, share), F32),
@@ -568,6 +630,12 @@
             dma((pairs,)),
             dma((2 * n_head,)),
             dma((n_head,)),
+            dma((n_head, 8)),
+            dma((n_head, 8)),
+            dma((n_head, 8)),
+            dma((n_head, 8)),
+            dma((n_head, 8)),
+            dma((n_head, 8)),
             dma((users, n_head)),
             dma((users, n_head)),
         ],
@@ -620,7 +688,7 @@
     )
     out_specs = (P("grp", "ctx", "head"), P("grp", ("ctx", "head")))
     return jax.shard_map(
-        functools.partial(local, mesh.shape["ctx"], mesh.shape["head"]),
+        functools.partial(local, mesh.shape["grp"], mesh.shape["ctx"], mesh.shape["head"]),
         mesh=mesh,
         in_specs=in_specs,
         out_specs=out_specs,

time: 25.2 us -> 27.2 us (1.079)
  Pallas kernels: 24.4 us -> 26.4 us
    pallas_call x1, Pallas kernels: 23.6 us -> 25.6 us  [local(): pl.pallas_call(functools.partial(kernel, n_grp, n_ctx, n_head, chunk), ou...]
where the time goes in v6:
time: 27.2 us; the launch traced here: 27.1 us
  Pallas kernels  26.4 us (97%)
  between operations  0.64 us (2%)
    pallas_call x1, Pallas kernels, local(): pl.pallas_call(functools.partial(kernel, n_grp, n_ctx, n_head, chunk), ou...  25.6 us
    pallas_call x1, Pallas kernels, local(): pl.pallas_call(results, out_shape=(jax.ShapeDtypeStruct(history_out.shape...  0.82 us

profile of v6, /device:TPU:0, one launch (start us, length us, event | category | flops | bytes accessed | tf_op | source)
XLA Modules:
  0.0 27.1 jit_solution(14395627645106271123)
XLA Ops:
  0.6 25.6 %shard_map.122 = (bf16[2,512,256]{2,1,0:T(8,128)(2,1)S(1)}, f32[2,32]{1,0:T(2,128)S(1)}) custom-call(s32[2]{0:T(128)} %hl.1, bf16[2,512,256]{2,1,0:T(8,128)(2,1)} %be_h.1, s32[2,512]{1,0:T(2,128)} %mk_h.1, f32[2,2,512]{2,1,0:T(2,128)} %ld_h.1, bf16[2,128,256]{2,1,0:T(8,128)(2,1)} %ce_h.1, bf16[256,1024]{1,0:T(8,128)(2,1)} %iw_h.1, f32[1,1024]{1,0:T(1,128)} %bitcast.3, ...), custom_call_target="tpu_custom_call" | custom-call | flops 2684354560 | bytes 6291456 | tf_op jit(solution)/shard_map/pallas_call | solution.py:588
  26.3 0.8 %shard_map.123 = (bf16[2,512,256]{2,1,0:T(8,128)(2,1)}, f32[2,32]{1,0:T(2,128)}) custom-call(bf16[2,512,256]{2,1,0:T(8,128)(2,1)S(1)} %get-tuple-element.4.hist_i, f32[2,32]{1,0:T(2,128)S(1)} %get-tuple-element.5.score_i), custom_call_target="tpu_custom_call" | custom-call | bytes 1048576 | tf_op jit(solution)/shard_map/pallas_call | solution.py:661

commit v7 on v5

--- a/solution.py
+++ b/solution.py
@@ -81,6 +81,9 @@
     x_out,
     feat,
     feat_in,
+    h_sum,
+    h_out,
+    h_in,
     load_sem,
     t_send,
     t_recv,
@@ -92,6 +95,8 @@
     r_recv,
     f_send,
     f_recv,
+    h_send,
+    h_recv,
 ):
     users, span, _ = be.shape
     cand = ce.shape[1]
@@ -149,9 +154,6 @@
 
     sibling = hm + 1 - 2 * core
     rank_copies = []
-    for k in range(CORES, n_head, CORES):
-        rank_copies.append(rank_copy(hm, lax.rem(hm + k, n_head), k, rf_h))
-        rank_copies[-1].start()
     rank_copies.append(rank_copy(hm, sibling, 0, rf_h))
     rank_copies[-1].start()
 
@@ -383,6 +385,10 @@
     for u in range(1, users):
         far_relay(u, False)
 
+    chips = n_head // CORES
+    chip = hm // CORES
+    rank_copy(sibling, sibling, 0).wait_recv()
+
     def candidates(u):
         rows = slice(u * cand, (u + 1) * cand)
         for h in range(heads):
@@ -393,17 +399,43 @@
             read = mm(cand_q[rows, hc], state.astype(BF16))
             scale = lax.rsqrt(jnp.mean(read * read, axis=-1, keepdims=True) + EPS)
             feat[u, :, hc] = (read * scale * out_gain[:, hc] + own[rows, hc]).astype(BF16)
-        for k in range(1, n_head):
-            feat_copy(u, k).start()
-
-    def feat_copy(u, k):
-        target = lax.rem(hm + k, n_head)
+        for x in range(chips):
+            feat_copy(u, x).start()
+
+    def feat_copy(u, x):
+        row = (CORES * x + 1 - core) * share
         return pltpu.make_async_remote_copy(
-            src_ref=feat.at[u, pl.ds(pl.multiple_of(target * share, share), share), :],
-            dst_ref=feat_in.at[hm, u],
-            send_sem=f_send.at[u, k],
-            recv_sem=f_recv.at[u, hm],
-            device_id={"head": target},
+            src_ref=feat.at[u, pl.ds(pl.multiple_of(row, share), share), :],
+            dst_ref=feat_in.at[u, x],
+            send_sem=f_send.at[u, x],
+            recv_sem=f_recv.at[u, x],
+            device_id={"head": sibling},
+            device_id_type=MESH,
+        )
+
+    def chip_sums(u):
+        rows = []
+        for x in range(chips):
+            row = (CORES * x + core) * share
+            rows.append(feat[u, pl.ds(pl.multiple_of(row, share), share), :])
+        part = mm(jnp.concatenate(rows, axis=0), rank[hm])
+        for x in range(chips):
+            feat_copy(u, x).wait_recv()
+        part = part + mm(feat_in[u].reshape(chips * share, cols), rank[sibling])
+        part = part.reshape(chips, share, part.shape[1])
+        h_sum[u] = part
+        h_out[u] = part.astype(BF16)
+        for k in range(1, chips):
+            sum_copy(u, k).start()
+
+    def sum_copy(u, k):
+        to = lax.rem(chip + k, chips)
+        return pltpu.make_async_remote_copy(
+            src_ref=h_out.at[u, to],
+            dst_ref=h_in.at[u, chip],
+            send_sem=h_send.at[u, k],
+            recv_sem=h_recv.at[u, chip],
+            device_id={"head": CORES * to + core},
             device_id_type=MESH,
         )
 
@@ -427,34 +459,28 @@
         candidates(u)
         if u + 1 < users:
             attention(u + 1)
-            histories(u)
-
-    for k in range(CORES, n_head, CORES):
-        src = lax.rem(hm + n_head - k, n_head)
-        rank_copy(src, sibling, k).wait_recv()
-        rank_copies.append(rank_copy(src, sibling, n_head + k))
-        rank_copies[-1].start()
-
+        else:
+            for v in range(users - 1):
+                histories(v)
+        chip_sums(u)
     histories(users - 1)
 
-    mine = feat[:, pl.ds(pl.multiple_of(hm * share, share), share), :]
-    hidden = mm(mine.reshape(users * share, cols), rank[hm])
-    rank_copy(sibling, sibling, 0).wait_recv()
-    for k in range(CORES, n_head, CORES):
-        src = lax.rem(sibling + n_head - k, n_head)
-        rank_copy(src, sibling, n_head + k).wait_recv()
-    for k in range(1, n_head):
-        src = lax.rem(hm + n_head - k, n_head)
-        for u in range(users):
+    totals = []
+    for u in range(users):
+        total = h_sum[u, chip]
+        for k in range(1, chips):
+            src = lax.rem(chip + chips - k, chips)
             pltpu.make_async_remote_copy(
-                src_ref=feat_in.at[src, u],
-                dst_ref=feat_in.at[src, u],
-                send_sem=f_send.at[u, k],
-                recv_sem=f_recv.at[u, src],
-                device_id={"head": src},
+                src_ref=h_in.at[u, src],
+                dst_ref=h_in.at[u, src],
+                send_sem=h_send.at[u, k],
+                recv_sem=h_recv.at[u, src],
+                device_id={"head": CORES * src + core},
                 device_id_type=MESH,
             ).wait_recv()
-        hidden = hidden + mm(feat_in[src].reshape(users * share, cols), rank[src])
+            total = total + h_in[u, src].astype(F32)
+        totals.append(total)
+    hidden = jnp.concatenate(totals, axis=0)
     second = r2[...].astype(F32)
     acted = silu(hidden)
     summed = acted[:, 0:128] * second[0:1, :]
@@ -465,8 +491,10 @@
     for cp in t_copies + rank_copies:
         cp.wait_send()
     for u in range(users):
-        for k in range(1, n_head):
-            feat_copy(u, k).wait_send()
+        for x in range(chips):
+            feat_copy(u, x).wait_send()
+        for k in range(1, chips):
+            sum_copy(u, k).wait_send()
     if n_ctx > 1:
 
         @pl.when(me < last)
@@ -558,7 +586,10 @@
             pltpu.VMEM((pairs, DH, DH), wire),
             pltpu.VMEM((pairs, DH, DH), wire),
             pltpu.VMEM((users, cand, cols), BF16),
-            pltpu.VMEM((n_head, users, share, cols), BF16),
+            pltpu.VMEM((users, n_head // CORES, share, cols), BF16),
+            pltpu.VMEM((users, n_head // CORES, share, hidden), F32),
+            pltpu.VMEM((users, n_head // CORES, share, hidden), BF16),
+            pltpu.VMEM((users, n_head // CORES, share, hidden), BF16),
             dma((13,)),
             dma((n_ctx,)),
             dma((n_ctx,)),
@@ -568,6 +599,8 @@
             dma((pairs,)),
             dma((2 * n_head,)),
             dma((n_head,)),
+            dma((users, n_head)),
+            dma((users, n_head)),
             dma((users, n_head)),
             dma((users, n_head)),
         ],

time: 25.2 us -> 27.4 us (1.087)
  Pallas kernels: 24.4 us -> 26.6 us
    pallas_call x1, Pallas kernels: 23.6 us -> 25.8 us  [local(): pl.pallas_call(functools.partial(kernel, n_ctx, n_head, chunk), out_shape...]
where the time goes in v7:
time: 27.4 us; the launch traced here: 27.2 us
  Pallas kernels  26.6 us (97%)
  between operations  0.64 us (2%)
    pallas_call x1, Pallas kernels, local(): pl.pallas_call(functools.partial(kernel, n_ctx, n_head, chunk), out_shape...  25.8 us
    pallas_call x1, Pallas kernels, local(): pl.pallas_call(results, out_shape=(jax.ShapeDtypeStruct(history_out.shape...  0.82 us

profile of v7, /device:TPU:0, one launch (start us, length us, event | category | flops | bytes accessed | tf_op | source)
XLA Modules:
  0.0 27.2 jit_solution(3113997970922265542)
XLA Ops:
  0.6 25.8 %shard_map.122 = (bf16[2,512,256]{2,1,0:T(8,128)(2,1)S(1)}, f32[2,32]{1,0:T(2,128)S(1)}) custom-call(s32[2]{0:T(128)} %hl.1, bf16[2,512,256]{2,1,0:T(8,128)(2,1)} %be_h.1, s32[2,512]{1,0:T(2,128)} %mk_h.1, f32[2,2,512]{2,1,0:T(2,128)} %ld_h.1, bf16[2,128,256]{2,1,0:T(8,128)(2,1)} %ce_h.1, bf16[256,1024]{1,0:T(8,128)(2,1)} %iw_h.1, f32[1,1024]{1,0:T(1,128)} %bitcast.3, ...), custom_call_target="tpu_custom_call" | custom-call | flops 2684354560 | bytes 6291456 | tf_op jit(solution)/shard_map/pallas_call | solution.py:554
  26.4 0.8 %shard_map.123 = (bf16[2,512,256]{2,1,0:T(8,128)(2,1)}, f32[2,32]{1,0:T(2,128)}) custom-call(bf16[2,512,256]{2,1,0:T(8,128)(2,1)S(1)} %get-tuple-element.4.hist_i, f32[2,32]{1,0:T(2,128)S(1)} %get-tuple-element.5.score_i), custom_call_target="tpu_custom_call" | custom-call | bytes 1048576 | tf_op jit(solution)/shard_map/pallas_call | solution.py:626

commit v8 on v5

--- a/solution.py
+++ b/solution.py
@@ -422,34 +422,38 @@
                 if c + 1 < chunks:
                     state = state * fades[c][p : p + 1, :] + lst[p, c]
 
+    def pass_on():
+        for k in range(CORES, n_head, CORES):
+            src = lax.rem(hm + n_head - k, n_head)
+            rank_copy(src, sibling, k).wait_recv()
+            rank_copies.append(rank_copy(src, sibling, n_head + k))
+            rank_copies[-1].start()
+
     for u in range(users):
+        if u == users - 1:
+            pass_on()
         far_relay(u, True)
         candidates(u)
         if u + 1 < users:
             attention(u + 1)
             histories(u)
 
-    for k in range(CORES, n_head, CORES):
-        src = lax.rem(hm + n_head - k, n_head)
-        rank_copy(src, sibling, k).wait_recv()
-        rank_copies.append(rank_copy(src, sibling, n_head + k))
-        rank_copies[-1].start()
-
     histories(users - 1)
 
     mine = feat[:, pl.ds(pl.multiple_of(hm * share, share), share), :]
     hidden = mm(mine.reshape(users * share, cols), rank[hm])
     rank_copy(sibling, sibling, 0).wait_recv()
-    for k in range(CORES, n_head, CORES):
-        src = lax.rem(sibling + n_head - k, n_head)
-        rank_copy(src, sibling, n_head + k).wait_recv()
-    for k in range(1, n_head):
-        src = lax.rem(hm + n_head - k, n_head)
+    direct = [lax.rem(hm + n_head - k, n_head) for k in range(CORES, n_head, CORES)]
+    passed = [lax.rem(sibling + n_head - k, n_head) for k in range(CORES, n_head, CORES)]
+    for i, src in enumerate([sibling] + direct + passed):
+        if i > len(direct):
+            k = CORES * (i - len(direct))
+            rank_copy(src, sibling, n_head + k).wait_recv()
         for u in range(users):
             pltpu.make_async_remote_copy(
                 src_ref=feat_in.at[src, u],
                 dst_ref=feat_in.at[src, u],
-                send_sem=f_send.at[u, k],
+                send_sem=f_send.at[u, 0],
                 recv_sem=f_recv.at[u, src],
                 device_id={"head": src},
                 device_id_type=MESH,

time: 25.2 us -> 25.2 us (level)
  no operation moved by 1% of the time
where the time goes in v8:
time: 25.2 us; the launch traced here: 25.1 us
  Pallas kernels  24.4 us (97%)
  between operations  0.64 us (3%)
    pallas_call x1, Pallas kernels, local(): pl.pallas_call(functools.partial(kernel, n_ctx, n_head, chunk), out_shape...  23.6 us
    pallas_call x1, Pallas kernels, local(): pl.pallas_call(results, out_shape=(jax.ShapeDtypeStruct(history_out.shape...  0.82 us

profile of v8, /device:TPU:0, one launch (start us, length us, event | category | flops | bytes accessed | tf_op | source)
XLA Modules:
  0.0 25.1 jit_solution(1651666407500048976)
XLA Ops:
  0.6 23.6 %shard_map.122 = (bf16[2,512,256]{2,1,0:T(8,128)(2,1)S(1)}, f32[2,32]{1,0:T(2,128)S(1)}) custom-call(s32[2]{0:T(128)} %hl.1, bf16[2,512,256]{2,1,0:T(8,128)(2,1)} %be_h.1, s32[2,512]{1,0:T(2,128)} %mk_h.1, f32[2,2,512]{2,1,0:T(2,128)} %ld_h.1, bf16[2,128,256]{2,1,0:T(8,128)(2,1)} %ce_h.1, bf16[256,1024]{1,0:T(8,128)(2,1)} %iw_h.1, f32[1,1024]{1,0:T(1,128)} %bitcast.3, ...), custom_call_target="tpu_custom_call" | custom-call | flops 2684354560 | bytes 6291456 | tf_op jit(solution)/shard_map/pallas_call | solution.py:530
  24.2 0.8 %shard_map.123 = (bf16[2,512,256]{2,1,0:T(8,128)(2,1)}, f32[2,32]{1,0:T(2,128)}) custom-call(bf16[2,512,256]{2,1,0:T(8,128)(2,1)S(1)} %get-tuple-element.4.hist_i, f32[2,32]{1,0:T(2,128)S(1)} %get-tuple-element.5.score_i), custom_call_target="tpu_custom_call" | custom-call | bytes 1048576 | tf_op jit(solution)/shard_map/pallas_call | solution.py:597
